TPU v7x, 32 devices: a whole 2x2x4 slice. The times are simulated.
32 devices in a mesh: row: 8 (over z, x), col: 2 (over core), vec: 2 (over y).
Axes of the slice: x: 2, y: 2, z: 4, core: 2. Of those that a mesh axis runs over, the one named last changes fastest.
Arguments:
- vectors: bfloat16 [131072, 256], P(('row', 'col'), 'vec'), parts along dimension 1, may hold values from -6 to 6
- tile_blocks: bfloat16 [8, 2, 32, 256, 256], P('row', 'col'), may hold values from -0.375 to 0.375
- block_rows: int32 [8, 2, 32], P('row', 'col'), may hold values from 0 to 63, as said below
- block_cols: int32 [8, 2, 32], P('row', 'col'), may hold values from 0 to 255, as said below
- counts: int32 [8, 2], P('row', 'col'), may hold values from 1 to 32, as said below
Outputs:
- filtered: bfloat16 [131072, 256], P(('row', 'col'), 'vec'), parts along dimension 1
There are 2 independent parts, one for each index of `vec`. A program takes and returns all parts, laid end to end along the dimension named above; an argument that names none is the same for every part. Nothing has to cross between parts.
Inputs may be any that keep to these rules, and one draw needn't show every extreme that they name: The pairs (block_rows, block_cols // 32) of the 32 slots of one tile are all distinct. Within one tile, all slots whose block columns lie in the same group of 32 (same block_cols // 32) name the same block column. `counts`: some tile uses all 32 slots.
All inputs are finite; a program needn't handle non-finite values.
Results may differ from a plain program's by a relative error of at most 0.015.
Values may be sent and summed in bfloat16 or wider, within the bound.
No kernel may reach another device: no remote copies, remote signals or barrier semaphores. Data moves between devices by JAX's collectives and lax.ppermute only.
A program may use at most 64 MiB of HBM per device.

v0:
```python
import functools
import typing

import jax
import jax.numpy as jnp
from jax import lax
from jax.experimental import pallas as pl
from jax.experimental.pallas import tpu as pltpu
from jax.sharding import PartitionSpec as P

DEGREE = 3

center_value = 0.5
half_width = 2.0

VMEM = pltpu.VMEM
SMEM = pltpu.SMEM
HBM = pltpu.HBM
DMA = pltpu.SemaphoreType.DMA
LANES = 128
FEW = 4
MANY = 4
HEAD = 8
STRIDE = 4
FIRST = 1
LAST = 2


def spec(space):
    return pl.BlockSpec(memory_space=space)


def params(mib):
    return pltpu.CompilerParams(vmem_limit_bytes=mib * 1024 * 1024)


def round_up(n, step):
    return (n + step - 1) // step * step


class Layout(typing.NamedTuple):
    slots: int
    sends: int
    loads: int
    sent_at: int
    load_at: int
    bare_at: int
    size: int


def layout_for(slot_count, n_row, piece_blocks):
    slots = round_up(slot_count, MANY) + MANY
    sends = round_up(2 * n_row * n_row, FEW) + FEW
    sent_at = HEAD + STRIDE * 2 * slots
    load_at = sent_at + STRIDE * 2 * sends
    bare_at = load_at + 2 * (slot_count + 1)
    size = round_up(bare_at + piece_blocks, 8 * LANES)
    return Layout(slots, sends, slot_count + 1, sent_at, load_at, bare_at, size)


def plan_kernel(
    n_row,
    piece_blocks,
    lay,
    place,
    wanted_a,
    wanted_b,
    meta_a,
    meta_b,
    own,
    other,
    out,
    count,
    asked,
    seen,
    sems,
):
    slot_count = (meta_a.shape[0] - 1) // 2

    def put(at, *values):
        for i, value in enumerate(values):
            out[at + i] = value

    def scan(tile, meta):
        used = meta[2 * slot_count]

        def step(s, carry):
            ends, sent, load = carry
            row = meta[s]
            piece = meta[slot_count + s] // piece_blocks
            live = s < used
            half = row // piece_blocks
            local = row - half * piece_blocks
            lower = half == 0
            part = jnp.where(lower, tile, 1 - tile)
            at = HEAD + STRIDE * (part * lay.slots + jnp.where(lower, ends[0], ends[1]))
            base = half * lay.size
            put(base + at, s, local, piece)
            found = jnp.where(live, count[row], 0)

            @pl.when(found > 0)
            def _():
                for core in range(2):
                    mine = tile if core == 0 else 1 - tile
                    side = half if core == 0 else 1 - half
                    first = core * lay.size
                    out[first + lay.load_at + mine * lay.loads + load] = s

                    @pl.loop(0, found)
                    def _(j):
                        put(
                            first + lay.sent_at + STRIDE * (mine * lay.sends + sent + j),
                            mine * lay.loads + load,
                            2 * asked[row * n_row + j] + side,
                            piece,
                            jnp.where(j == 0, FIRST, 0),
                        )

            one = live.astype(jnp.int32)
            ends = (ends[0] + jnp.where(lower, one, 0), ends[1] + jnp.where(lower, 0, one))
            return ends, sent + found, load + jnp.where(found > 0, 1, 0)

        zero = jnp.int32(0)
        ends, sent, load = lax.fori_loop(0, slot_count, step, ((zero, zero), zero, zero))
        for core in range(2):
            mine = tile if core == 0 else 1 - tile
            base = core * lay.size
            for i, (at, begin, end, unit, spare) in enumerate(
                (
                    (HEAD, mine * lay.slots, ends[core], MANY, piece_blocks),
                    (lay.sent_at, mine * lay.sends, sent, FEW, 2 * n_row),
                )
            ):
                for u in range(unit - 1):
                    put(base + at + STRIDE * (begin + end + u), 0, spare, 0, 0)
                out[base + 2 * i + mine] = begin + (end + unit - 1) // unit * unit
            out[base + 4 + mine] = mine * lay.loads + load

    def mark(core):
        base = core * lay.size
        for b in range(piece_blocks + 1):
            seen[b] = 0
        for part in range(2):

            @pl.loop(part * lay.slots, out[base + part])
            def _(i):
                entry = base + HEAD + STRIDE * i
                row = out[entry + 1]
                out[entry + 3] = jnp.where(seen[row] == 0, FIRST, 0)
                seen[row] = entry

        def close(b, bare):
            entry = seen[b]
            out[base + lay.bare_at + bare] = b

            @pl.when(entry > 0)
            def _():
                out[entry + 3] = out[entry + 3] + LAST

            return bare + jnp.where(entry == 0, 1, 0)

        out[base + 6] = lax.fori_loop(0, piece_blocks, close, jnp.int32(0))
        out[base + 7] = core

    @pl.when(place[1] == 0)
    def _():
        for row in range(2 * piece_blocks):
            count[row] = 0
        for half, wanted in enumerate((wanted_a, wanted_b)):
            for k in range(n_row):
                row = half * piece_blocks + wanted[k, 0]
                number = count[row]
                asked[row * n_row + number] = k
                count[row] = number + 1
        scan(0, meta_a)
        scan(1, meta_b)
        for core in range(2):
            mark(core)
        copies = [
            pltpu.make_async_copy(out.at[pl.ds(core * lay.size, lay.size)], target, sems.at[core])
            for core, target in enumerate((own, other))
        ]
        for copy in copies:
            copy.start()
        for copy in copies:
            copy.wait()


def settle_kernel(place, own, handed, out, sem):
    for half, source in enumerate((own, handed)):

        @pl.when(place[1] == half)
        def _():
            copy = pltpu.make_async_copy(source, out, sem)
            copy.start()
            copy.wait()


def pick_kernel(n_row, block_size, wanted, vectors, out, sems):
    def fetch(k):
        at = pl.multiple_of(wanted[k, 0] * block_size, block_size)
        return pltpu.make_async_copy(vectors.at[pl.ds(at, block_size)], out.at[k], sems.at[k])

    for k in range(n_row):
        fetch(k).start()
    for k in range(n_row):
        fetch(k).wait()


def pack_kernel(place, picked, picked_b, out, held, sems):
    n_row, _, width = picked.shape
    middle = width // 2

    def put(k):
        return pltpu.make_async_copy(held.at[k], out.at[k], sems.at[k])

    for half in range(2):

        @pl.when(place[1] == half)
        def _():
            part = slice(half * middle, (half + 1) * middle)
            for k in range(n_row):
                held[k] = jnp.concatenate([picked[k, :, part], picked_b[k, :, part]], axis=1)
                put(k).start()

    for k in range(n_row):
        put(k).wait()


def fetches(plan, base, stride, ends, part, tiles, blocks, sems):
    def copy(tile, i):
        slot = plan[base + stride * i]
        return pltpu.make_async_copy(tile.at[slot], blocks.at[i], sems.at[i])

    def start():
        for side, tile in enumerate(tiles):

            @pl.loop(side * part, plan[ends + side])
            def _(i):
                copy(tile, i).start()

    def wait(i):
        copy(tiles[0], i).wait()

    return start, wait


def load_kernel(plan, tile_a, array, blocks, held, sems, held_sem):
    whole = pltpu.make_async_copy(array, held, held_sem)
    whole.start()
    start, wait = fetches(plan, HEAD, STRIDE, 0, 0, (tile_a,), blocks, sems)
    start()

    @pl.loop(0, plan[0])
    def _(i):
        wait(i)

    whole.wait()


def each_product(plan, base, ends, part, block_of, pieces, use, then=None, before=None):
    unroll = MANY if base == HEAD else FEW

    for side in range(2):

        @pl.loop(side * part // unroll, plan[ends + side] // unroll)
        def _(j):
            step = [(unroll * j + u, base + STRIDE * (unroll * j + u)) for u in range(unroll)]
            if before is not None:
                for i, entry in step:
                    before(side, i, entry)
            for i, entry in step:
                block = block_of(side, i, entry)
                piece = pieces[side][plan[entry + 2]]
                use(entry, jnp.dot(block, piece, preferred_element_type=jnp.float32))
            if then is not None:
                for i, entry in step:
                    then(entry)


def add_products(plan, base, ends, part, block_of, pieces, total, before=None):
    def use(entry, value):
        total[plan[entry + 1]] += value

    each_product(plan, base, ends, part, block_of, pieces, use, before=before)


def split_sides(pieces, vec):
    middle = vec.shape[-1] // 2
    column = lax.broadcasted_iota(jnp.int32, (1, vec.shape[-1]), 1)
    for side in range(2):
        keep = jnp.where((column // middle) == side, 1.0, 0.0).astype(jnp.bfloat16)
        for p in range(vec.shape[1]):
            vec[side, p] = pieces[p] * keep


def joined(total, k):
    one, two = total[2 * k], total[2 * k + 1]
    low = lax.broadcasted_iota(jnp.int32, one.shape, 1) < one.shape[1] // 2
    return jnp.where(low, one, two) + pltpu.roll(
        jnp.where(low, two, one), one.shape[1] // 2, axis=1
    )


def first_sent_kernel(
    lay, plan, tile_a, tile_b, pieces, start, out, blocks, vec, total, held, held_sem, sems
):
    n_row = out.shape[0]
    begin, wait = fetches(plan, lay.load_at, 1, 4, lay.loads, (tile_a, tile_b), blocks, sems)
    begin()
    copy = pltpu.make_async_copy(start, held, held_sem)
    copy.start()
    split_sides(pieces, vec)
    total[...] = jnp.zeros_like(total)

    def before(side, i, entry):
        @pl.when(plan[entry + 3] == FIRST)
        def _():
            wait(plan[entry])

    add_products(
        plan,
        lay.sent_at,
        2,
        lay.sends,
        lambda side, i, entry: blocks[plan[entry]],
        (vec.at[0], vec.at[1]),
        total,
        before,
    )
    copy.wait()
    for k in range(n_row):
        value = joined(total, k) - center_value * held[k].astype(jnp.float32)
        out[k] = (value / half_width).astype(jnp.bfloat16)


def second_sent_kernel(
    lay, plan, blocks, pieces, current, previous, out, vec, total, held, held_sem, ready, out_sems
):
    n_row = out.shape[0]
    copy = pltpu.make_async_copy(previous, held, held_sem)
    copy.start()
    split_sides(pieces, vec)
    total[...] = jnp.zeros_like(total)
    add_products(
        plan,
        lay.sent_at,
        2,
        lay.sends,
        lambda side, i, entry: blocks[plan[entry]],
        (vec.at[0], vec.at[1]),
        total,
    )
    copy.wait()

    def put(k):
        return pltpu.make_async_copy(ready.at[k], out.at[k], out_sems.at[k])

    for k in range(n_row):
        value = joined(total, k) - center_value * current[k].astype(jnp.float32)
        ready[k] = (value - held[k].astype(jnp.float32)).astype(jnp.bfloat16)
        put(k).start()
    for k in range(n_row):
        put(k).wait()


def whole_columns(half, mine, other, vec, at):
    n_row, _, width = mine.shape
    middle = width // 2

    @pl.when(half == 0)
    def _():
        @pl.loop(0, n_row)
        def _(p):
            one, two = mine[p], other[p]
            vec[0, p, :, at : at + width] = jnp.concatenate([one[:, :middle], two[:, middle:]], axis=1)
            vec[1, p, :, at : at + width] = jnp.concatenate([one[:, middle:], two[:, :middle]], axis=1)

    @pl.when(half != 0)
    def _():
        @pl.loop(0, n_row)
        def _(p):
            one, two = mine[p], other[p]
            vec[0, p, :, at : at + width] = jnp.concatenate([two[:, middle:], one[:, :middle]], axis=1)
            vec[1, p, :, at : at + width] = jnp.concatenate([two[:, :middle], one[:, middle:]], axis=1)


def early_kernel(
    lay,
    plan,
    tile_a,
    tile_b,
    q1,
    q1_other,
    q2,
    q2_other,
    vectors,
    base,
    vec,
    total,
    own,
    blocks,
    sem,
    sems,
    row_sems,
):
    width = vectors.shape[1]
    piece_blocks, block_size, _ = base.shape
    copy = pltpu.make_async_copy(vectors, own, sem)
    copy.start()
    begin, wait = fetches(plan, HEAD, STRIDE, 0, lay.slots, (tile_a, tile_b), blocks, sems)
    begin()
    whole_columns(plan[7], q1, q1_other, vec, 0)
    whole_columns(plan[7], q2, q2_other, vec, width)
    copy.wait()

    def rows(b):
        return pl.ds(pl.multiple_of(b * block_size, block_size), block_size)

    def put(b):
        return pltpu.make_async_copy(own.at[rows(b)], base.at[b], row_sems.at[b])

    @pl.loop(0, piece_blocks)
    def _(b):
        value = own[rows(b), :].astype(jnp.float32)
        total[b, :, :width] = -center_value * value
        total[b, :, width:] = -value

    add_products(
        plan,
        HEAD,
        0,
        lay.slots,
        lambda side, i, entry: blocks[i],
        (vec.at[0], vec.at[1]),
        total,
        lambda side, i, entry: wait(i),
    )

    @pl.loop(0, piece_blocks)
    def _(b):
        first = (total[b, :, :width] / half_width).astype(jnp.bfloat16).astype(jnp.float32)
        second = total[b, :, width:] - center_value * first
        second = second.astype(jnp.bfloat16).astype(jnp.float32)
        own[rows(b), :] = (-center_value * second - first).astype(jnp.bfloat16)
        put(b).start()

    @pl.loop(0, piece_blocks)
    def _(b):
        put(b).wait()


def last_kernel(
    lay, plan, blocks, tile_b, mine, other, base, out, vec, total, own, blocks_b, sems, row_sems
):
    piece_blocks = base.shape[0]
    begin = lay.slots

    def fetch(i):
        slot = plan[HEAD + STRIDE * i]
        return pltpu.make_async_copy(tile_b.at[slot], blocks_b.at[i - begin], sems.at[i - begin])

    @pl.loop(begin, plan[1])
    def _(i):
        fetch(i).start()

    def put(source, b):
        return pltpu.make_async_copy(source.at[b], out.at[b], row_sems.at[b])

    @pl.loop(0, plan[6])
    def _(i):
        b = plan[lay.bare_at + i]
        put(base, b).start()

    whole_columns(plan[7], mine, other, vec, 0)

    def use(entry, value):
        row = plan[entry + 1]
        marks = plan[entry + 3]
        start = base[jnp.minimum(row, piece_blocks - 1)].astype(jnp.float32)
        value = jnp.where(lax.rem(marks, LAST) == FIRST, start, total[row]) + value
        total[row] = value
        own[row] = value.astype(jnp.bfloat16)

    def then(entry):
        @pl.when(plan[entry + 3] >= LAST)
        def _():
            put(own, plan[entry + 1]).start()

    def block_of(side, i, entry):
        return blocks[i] if side == 0 else blocks_b[i - begin]

    def before(side, i, entry):
        if side == 1:
            fetch(i).wait()

    each_product(
        plan, HEAD, 0, lay.slots, block_of, (vec.at[0], vec.at[1]), use, then, before
    )

    @pl.loop(0, piece_blocks)
    def _(b):
        put(own, b).wait()


def after(value, *others):
    return lax.optimization_barrier((value, *others))[0]


def call(kernel, out, args, spaces, scratch, mib, name, estimate=None):
    args = [
        pltpu.with_memory_space_constraint(arg, space) if space in (VMEM, HBM) or tied else arg
        for arg, (space, tied) in zip(args, spaces)
    ]
    return pl.pallas_call(
        kernel,
        out_shape=[space(shape, dtype) for shape, dtype, space in out],
        in_specs=[spec(space) for space, _ in spaces],
        out_specs=[spec(space) for _, _, space in out],
        scratch_shapes=scratch,
        compiler_params=params(mib),
        cost_estimate=estimate,
        name=name,
    )(*args)


HERE = (VMEM, True)
FAR = (HBM, True)
LIST = (SMEM, True)
SCALARS = (SMEM, False)
ANYWHERE = (pl.ANY, False)


def on_pair(vectors, tile_blocks, block_rows, block_cols, counts):
    n_row = lax.axis_size("row")
    tile = tile_blocks[0, 0]
    slot_rows = block_rows[0, 0]
    slot_cols = block_cols[0, 0]
    used = counts[0]
    slot_count, block_size, _ = tile.shape
    width = vectors.shape[1]
    piece_blocks = vectors.shape[0] // block_size
    place = jnp.stack([lax.axis_index("row"), lax.axis_index("col")]).astype(jnp.int32)

    across = functools.partial(lax.ppermute, axis_name="col", perm=[(0, 1), (1, 0)])

    needed = jnp.max(
        jnp.where(
            slot_cols[None, :] // piece_blocks == jnp.arange(n_row)[:, None],
            slot_cols[None, :] % piece_blocks,
            0,
        ),
        axis=1,
        keepdims=True,
    )
    exchange = functools.partial(
        lax.all_to_all, axis_name="row", split_axis=0, concat_axis=0, tiled=True
    )
    meta = jnp.concatenate([slot_rows, slot_cols, used])
    meta_other = across(meta)
    wanted = after(exchange(jnp.broadcast_to(needed, (n_row, LANES))), meta_other, place)
    sent_shape = (n_row, block_size, width)
    (sent,) = call(
        functools.partial(pick_kernel, n_row, block_size),
        [(sent_shape, jnp.bfloat16, VMEM)],
        (wanted, vectors),
        (SCALARS, FAR),
        [DMA((n_row,))],
        2,
        "pick",
    )
    tile_other = across(tile)
    sent_other = across(sent)
    wanted_other = across(after(wanted, sent))
    packed = call(
        pack_kernel,
        [(sent_shape, jnp.bfloat16, HBM)],
        (place, sent, sent_other),
        (SCALARS, HERE, HERE),
        [VMEM(sent_shape, jnp.bfloat16), DMA((n_row,))],
        4,
        "pack",
    )[0]

    lay = layout_for(slot_count, n_row, piece_blocks)
    list_shape = ((lay.size,), jnp.int32)
    own_list, other_list = call(
        functools.partial(plan_kernel, n_row, piece_blocks, lay),
        [(*list_shape, HBM)] * 2,
        (place, wanted, after(wanted_other, packed), meta, meta_other),
        (SCALARS,) * 5,
        [
            SMEM((2 * lay.size,), jnp.int32),
            SMEM((2 * piece_blocks,), jnp.int32),
            SMEM((2 * piece_blocks * n_row,), jnp.int32),
            SMEM((piece_blocks + 1,), jnp.int32),
            DMA((2,)),
        ],
        2,
        "plan",
    )
    q1 = exchange(after(packed, own_list))
    plan = call(
        settle_kernel,
        [(*list_shape, SMEM)],
        (place, own_list, across(after(other_list, packed))),
        (SCALARS, ANYWHERE, ANYWHERE),
        [DMA],
        2,
        "settle",
    )[0]

    def load(cue, array):
        return call(
            load_kernel,
            [
                ((lay.slots, block_size, block_size), jnp.bfloat16, VMEM),
                (array.shape, array.dtype, VMEM),
            ],
            (after(plan, cue), tile, array),
            (LIST, FAR, FAR),
            [DMA((lay.slots,)), DMA],
            2,
            "load",
        )

    def cost(products, rows):
        size = block_size * width
        return pl.CostEstimate(
            flops=2 * products * block_size * size,
            bytes_accessed=2 * (products * block_size * block_size + 3 * rows * size),
            transcendentals=0,
        )

    sums = [
        VMEM((2, n_row, block_size, width), jnp.bfloat16),
        VMEM((2 * n_row + 1, block_size, width), jnp.float32),
    ]

    def first_blocks(*args):
        return call(
            functools.partial(first_sent_kernel, lay),
            [
                (sent_shape, jnp.bfloat16, VMEM),
                ((2 * lay.loads, block_size, block_size), jnp.bfloat16, VMEM),
            ],
            (plan, tile, tile_other, *args),
            (LIST, FAR, ANYWHERE, HERE, FAR),
            sums + [VMEM(sent_shape, jnp.bfloat16), DMA, DMA((2 * lay.loads,))],
            8,
            "sent",
            cost(n_row, n_row),
        )

    def second_blocks(*args):
        return call(
            functools.partial(second_sent_kernel, lay),
            [(sent_shape, jnp.bfloat16, HBM)],
            (plan, *args),
            (LIST, HERE, HERE, HERE, FAR),
            sums
            + [VMEM(sent_shape, jnp.bfloat16), DMA, VMEM(sent_shape, jnp.bfloat16), DMA((n_row,))],
            8,
            "sent",
            cost(n_row, n_row),
        )[0]

    base_shape = (piece_blocks, block_size, width)

    def early(*args):
        return call(
            functools.partial(early_kernel, lay),
            [(base_shape, jnp.bfloat16, HBM)],
            (plan, tile, tile_other, *args),
            (LIST, FAR, ANYWHERE, HERE, HERE, HERE, HERE, FAR),
            [
                VMEM((2, n_row, block_size, 2 * width), jnp.bfloat16),
                VMEM((piece_blocks + 1, block_size, 2 * width), jnp.float32),
                VMEM(vectors.shape, jnp.bfloat16),
                VMEM((2 * lay.slots, block_size, block_size), jnp.bfloat16),
                DMA,
                DMA((2 * lay.slots,)),
                DMA((piece_blocks,)),
            ],
            28,
            "early",
            cost(2 * slot_count, 2 * piece_blocks),
        )[0]

    def last(blocks, *args):
        rows = (piece_blocks + 1, block_size, width)
        (out,) = call(
            functools.partial(last_kernel, lay),
            [(base_shape, jnp.bfloat16, HBM)],
            (plan, blocks, tile_other, *args),
            (LIST, HERE, ANYWHERE, HERE, HERE, HERE),
            [
                VMEM((2, n_row, block_size, width), jnp.bfloat16),
                VMEM(rows, jnp.float32),
                VMEM(rows, jnp.bfloat16),
                VMEM((lay.slots, block_size, block_size), jnp.bfloat16),
                DMA((lay.slots,)),
                DMA((piece_blocks,)),
            ],
            14,
            "last",
            cost(slot_count, piece_blocks),
        )
        return out.reshape(vectors.shape)

    q1 = after(q1, plan)
    first_sent, blocks = first_blocks(q1, packed)
    q2 = exchange(first_sent)
    second_sent = second_blocks(blocks, q2, first_sent, packed)
    q1_other = across(after(q1, second_sent))
    q2_other = across(after(q2, second_sent))
    base = early(q1, q1_other, q2, q2_other, vectors)
    q3 = after(exchange(second_sent), base)
    q3_other = across(q3)
    blocks, base = load(q3, base)
    return last(blocks, q3, q3_other, base)


def on_any(vectors, tile_blocks, block_rows, block_cols, counts):
    n_row = lax.axis_size("row")
    n_col = lax.axis_size("col")
    tile_data = tile_blocks[0, 0]
    slot_rows = block_rows[0, 0]
    slot_cols = block_cols[0, 0]
    used = counts[0, 0]
    block_size = tile_data.shape[-1]
    width = vectors.shape[1]
    piece_blocks = vectors.shape[0] // block_size
    row_blocks = piece_blocks * n_col
    slot_count = tile_data.shape[0]
    live = (jnp.arange(slot_count) < used).astype(jnp.float32)
    onehot = (slot_rows[None, :] == jnp.arange(row_blocks)[:, None]).astype(jnp.float32) * live[
        None, :
    ]
    source_piece = slot_cols // piece_blocks
    offset = slot_cols % piece_blocks
    needed = jnp.max(
        jnp.where(source_piece[None, :] == jnp.arange(n_row)[:, None], offset[None, :], 0), axis=1
    )
    wanted = lax.all_to_all(
        needed.reshape(n_row, 1), "row", split_axis=0, concat_axis=0, tiled=True
    ).reshape(n_row)

    def apply_tiles(current):
        own_blocks = current.reshape(piece_blocks, block_size, width)
        outgoing = jnp.take(own_blocks, wanted, axis=0)
        received = lax.all_to_all(outgoing, "row", split_axis=0, concat_axis=0, tiled=True)
        vec_blocks = jnp.take(received, source_piece, axis=0)
        products = jnp.einsum(
            "sij,sjk->sik", tile_data, vec_blocks, preferred_element_type=jnp.float32
        )
        term = jnp.einsum("ls,sik->lik", onehot, products, precision=lax.Precision.HIGHEST)
        term = term.reshape(row_blocks * block_size, width)
        return lax.psum_scatter(
            term.astype(jnp.bfloat16), "col", scatter_dimension=0, tiled=True
        ).astype(jnp.float32)

    previous = vectors
    applied = apply_tiles(vectors)
    current = ((applied - center_value * previous.astype(jnp.float32)) / half_width).astype(
        jnp.bfloat16
    )
    for repeat in range(DEGREE - 1):
        applied = apply_tiles(current)
        following = (
            2.0 * (applied - center_value * current.astype(jnp.float32)) / half_width
            - previous.astype(jnp.float32)
        ).astype(jnp.bfloat16)
        previous, current = (current, following)
    return current


def solution(mesh):
    n_row, n_col = mesh.shape["row"], mesh.shape["col"]
    paired = n_col == 2 and n_row & (n_row - 1) == 0
    return jax.shard_map(
        on_pair if paired else on_any,
        mesh=mesh,
        in_specs=(
            P(("row", "col"), "vec"),
            P("row", "col", None, None, None),
            P("row", "col", None),
            P("row", "col", None),
            P("row", "col"),
        ),
        out_specs=P(("row", "col"), "vec"),
        check_vma=False,
    )
```

profile of v0, /device:TPU:0, one launch (start us, length us, event | category | flops | bytes accessed | tf_op | source)
XLA Modules:
  0.0 83.4 jit_solution(10443800049445701)
XLA Ops:
  1.2 0.7 broadcast_in_dim.21
  1.9 6.8 %all-to-all-start = ((s32[8,1,128]{2,1,0:T(1,128)}), s32[8,1,128]{2,1,0:T(1,128)S(1)}, u32[]{:S(2)}, u32[]{:S(2)}) async-start(s32[8,1,128]{2,1,0:T(1,128)} %broadcast_in_dim.21), calls=%async_computation | async-start | bytes 8192 | tf_op jit(solution)/shard_map/all_to_all | solution.py:561
  9.4 0.7 pad_add_fusion.1.meta_a
  10.4 0.8 collective-permute-done.meta_b
  11.2 3.9 %all-to-all-done = s32[8,1,128]{2,1,0:T(1,128)S(1)} async-done(((s32[8,1,128]{2,1,0:T(1,128)}), s32[8,1,128]{2,1,0:T(1,128)S(1)}, u32[]{:S(2)}, u32[]{:S(2)}) %all-to-all-start) | async-done | bytes 4128 | tf_op jit(solution)/shard_map/all_to_all | solution.py:561
  15.1 1.7 %pick.1.picked = bf16[8,256,128]{2,1,0:T(8,128)(2,1)S(1)} custom-call(s32[8,128]{1,0:T(8,128)S(1)} %bitcast.15, bf16[8192,128]{1,0:T(8,128)(2,1)} %vectors.3), custom_call_target="tpu_custom_call" | custom-call | tf_op jit(solution)/shard_map/pick/pallas_call | solution.py:515
  17.4 1.4 %collective-permute-done.2.picked_b = bf16[8,256,128]{2,1,0:T(8,128)(2,1)S(1)} collective-permute-done((bf16[8,256,128]{2,1,0:T(8,128)(2,1)S(1)}, bf16[8,256,128]{2,1,0:T(8,128)(2,1)S(1)}, u32[]{:S(2)}, u32[]{:S(2)}) %collective-permute-start.2) | collective-permute-done | bytes 524320 | tf_op jit(solution)/shard_map/ppermute | solution.py:573
  18.8 1.5 %pack.1.start.previous = bf16[8,256,128]{2,1,0:T(8,128)(2,1)} custom-call(s32[2]{0:T(128)S(1)} %pad_add_fusion.place, bf16[8,256,128]{2,1,0:T(8,128)(2,1)S(1)} %pick.1.picked, bf16[8,256,128]{2,1,0:T(8,128)(2,1)S(1)} %collective-permute-done.2.picked_b), custom_call_target="tpu_custom_call" | custom-call | tf_op jit(solution)/shard_map/pack/pallas_call | solution.py:515
  20.3 4.9 %plan.1 = (s32[2048]{0:T(1024)}, s32[2048]{0:T(1024)}) custom-call(s32[2]{0:T(128)S(1)} %pad_add_fusion.place, s32[8,128]{1,0:T(8,128)S(1)} %bitcast.17, s32[8,128]{1,0:T(8,128)S(1)} %collective-permute-done.1.wanted_b, s32[65]{0:T(128)S(1)} %pad_add_fusion.1.meta_a, s32[65]{0:T(128)S(1)} %collective-permute-done.meta_b), custom_call_target="tpu_custom_call" | custom-call | tf_op jit(solution)/shard_map/plan/pallas_call | solution.py:515
  25.3 3.5 %all-to-all-start.1 = ((bf16[8,256,128]{2,1,0:T(8,128)(2,1)}), bf16[8,256,128]{2,1,0:T(8,128)(2,1)S(1)}, u32[]{:S(2)}, u32[]{:S(2)}) async-start(bf16[8,256,128]{2,1,0:T(8,128)(2,1)} %pack.1.start.previous), calls=%async_computation.1 | async-start | bytes 1048576 | tf_op jit(solution)/shard_map/all_to_all | solution.py:602
  28.8 1.4 %collective-permute-done.3.handed = s32[2048]{0:T(1024)S(1)} collective-permute-done((s32[2048]{0:T(1024)}, s32[2048]{0:T(1024)S(1)}, u32[]{:S(2)}, u32[]{:S(2)}) %collective-permute-start.3) | collective-permute-done | bytes 8224 | tf_op jit(solution)/shard_map/ppermute | solution.py:606
  30.2 0.7 copy-done
  30.9 1.2 %settle.1.plan = s32[2048]{0:T(1024)S(4)} custom-call(s32[2]{0:T(128)S(1)} %pad_add_fusion.place, s32[2048]{0:T(1024)S(1)} %copy-done, s32[2048]{0:T(1024)S(1)} %collective-permute-done.3.handed), custom_call_target="tpu_custom_call" | custom-call | tf_op jit(solution)/shard_map/settle/pallas_call | solution.py:515
  32.2 7.4 %all-to-all-done.1.pieces.q1 = bf16[8,256,128]{2,1,0:T(8,128)(2,1)S(1)} async-done(((bf16[8,256,128]{2,1,0:T(8,128)(2,1)}), bf16[8,256,128]{2,1,0:T(8,128)(2,1)S(1)}, u32[]{:S(2)}, u32[]{:S(2)}) %all-to-all-start.1) | async-done | bytes 524320 | tf_op jit(solution)/shard_map/all_to_all | solution.py:602
  39.6 3.3 %sent.2 = (bf16[8,256,128]{2,1,0:T(8,128)(2,1)S(1)}, bf16[66,256,256]{2,1,0:T(8,128)(2,1)S(1)}) custom-call(s32[2048]{0:T(1024)S(4)} %settle.1.plan, bf16[32,256,256]{2,1,0:T(8,128)(2,1)} %bitcast.19, bf16[32,256,256]{2,1,0:T(8,128)(2,1)} %collective-permute-done.4.tile_b, bf16[8,256,128]{2,1,0:T(8,128)(2,1)S(1)} %all-to-all-done.1.pieces.q1, ...), custom_call_target="tpu_custom_call" | custom-call | flops 134217728 | bytes 2621440 | tf_op jit(solution)/shard_map/sent/pallas_call | solution.py:515
  42.9 15.1 %all_to_all.24.pieces.q2 = bf16[8,256,128]{2,1,0:T(8,128)(2,1)S(1)} all-to-all(bf16[8,256,128]{2,1,0:T(8,128)(2,1)S(1)} %get-tuple-element.30.current), channel_id=1, replica_groups=mesh['row'=8,'col'=2,'vec'=2] {'row'}, dimensions={0} | all-to-all | bytes 1048576 | tf_op jit(solution)/shard_map/all_to_all | solution.py:713
  58.0 2.5 %sent.3 = bf16[8,256,128]{2,1,0:T(8,128)(2,1)} custom-call(s32[2048]{0:T(1024)S(4)} %settle.1.plan, bf16[66,256,256]{2,1,0:T(8,128)(2,1)S(1)} %get-tuple-element.29.blocks, bf16[8,256,128]{2,1,0:T(8,128)(2,1)S(1)} %all_to_all.24.pieces.q2, bf16[8,256,128]{2,1,0:T(8,128)(2,1)S(1)} %get-tuple-element.30.current, bf16[8,256,128]{2,1,0:T(8,128)(2,1)} %pack.1.start.previous), custom_call_target="tpu_custom_call" | custom-call | flops 134217728 | bytes 2621440 | tf_op jit(solution)/shard_map/sent/pallas_call | solution.py:515
  60.5 3.7 %all-to-all-start.3 = ((bf16[8,256,128]{2,1,0:T(8,128)(2,1)}), bf16[8,256,128]{2,1,0:T(8,128)(2,1)S(1)}, u32[]{:S(2)}, u32[]{:S(2)}) async-start(bf16[8,256,128]{2,1,0:T(8,128)(2,1)} %sent.3), calls=%async_computation.3 | async-start | bytes 1048576 | tf_op jit(solution)/shard_map/all_to_all | solution.py:718
  64.7 1.4 %collective-permute-done.5.q1_other = bf16[8,256,128]{2,1,0:T(8,128)(2,1)S(1)} collective-permute-done((bf16[8,256,128]{2,1,0:T(8,128)(2,1)S(1)}, bf16[8,256,128]{2,1,0:T(8,128)(2,1)S(1)}, u32[]{:S(2)}, u32[]{:S(2)}) %collective-permute-start.5) | collective-permute-done | bytes 524320 | tf_op jit(solution)/shard_map/ppermute | solution.py:715
  66.1 0.7 collective-permute-done.6.q2_other
  66.9 7.1 %early.1.array = bf16[32,256,128]{2,1,0:T(8,128)(2,1)} custom-call(s32[2048]{0:T(1024)S(4)} %settle.1.plan, bf16[32,256,256]{2,1,0:T(8,128)(2,1)} %bitcast.20, bf16[32,256,256]{2,1,0:T(8,128)(2,1)} %collective-permute-done.4.tile_b, bf16[8,256,128]{2,1,0:T(8,128)(2,1)S(1)} %all-to-all-done.1.pieces.q1, ...), custom_call_target="tpu_custom_call" | custom-call | flops 1073741824 | bytes 20971520 | tf_op jit(solution)/shard_map/early/pallas_call | solution.py:515
  74.0 3.4 %all-to-all-done.3.mine = bf16[8,256,128]{2,1,0:T(8,128)(2,1)S(1)} async-done(((bf16[8,256,128]{2,1,0:T(8,128)(2,1)}), bf16[8,256,128]{2,1,0:T(8,128)(2,1)S(1)}, u32[]{:S(2)}, u32[]{:S(2)}) %all-to-all-start.3) | async-done | bytes 524320 | tf_op jit(solution)/shard_map/all_to_all | solution.py:718
  77.4 2.0 %load.1 = (bf16[36,256,256]{2,1,0:T(8,128)(2,1)S(1)}, bf16[32,256,128]{2,1,0:T(8,128)(2,1)S(1)}) custom-call(s32[2048]{0:T(1024)S(4)} %settle.1.plan, bf16[32,256,256]{2,1,0:T(8,128)(2,1)} %bitcast.21, bf16[32,256,128]{2,1,0:T(8,128)(2,1)} %early.1.array), custom_call_target="tpu_custom_call" | custom-call | tf_op jit(solution)/shard_map/load/pallas_call | solution.py:515
  79.4 4.0 %last.1 = bf16[32,256,128]{2,1,0:T(8,128)(2,1)} custom-call(s32[2048]{0:T(1024)S(4)} %settle.1.plan, bf16[36,256,256]{2,1,0:T(8,128)(2,1)S(1)} %get-tuple-element.35.blocks, bf16[32,256,256]{2,1,0:T(8,128)(2,1)} %collective-permute-done.4.tile_b, bf16[8,256,128]{2,1,0:T(8,128)(2,1)S(1)} %all-to-all-done.3.mine, ...), custom_call_target="tpu_custom_call" | custom-call | flops 536870912 | bytes 10485760 | tf_op jit(solution)/shard_map/last/pallas_call | solution.py:515
  (15 shorter events, 2.7 us)
Async XLA Ops:
  0.0 39.5 %collective-permute-start.4 = (bf16[32,256,256]{2,1,0:T(8,128)(2,1)}, bf16[32,256,256]{2,1,0:T(8,128)(2,1)}, u32[]{:S(2)}, u32[]{:S(2)}) collective-permute-start(bf16[32,256,256]{2,1,0:T(8,128)(2,1)} %bitcast.18), channel_id=1, source_target_pairs={{0,2},{2,0},{1,3},{3,1},{4,6},{6,4},{5,7},{7,5},{8,10},{10,8},{9,1... | collective-permute-start | bytes 12582920 | tf_op jit(solution)/shard_map/ppermute | solution.py:572
  1.9 13.2 %all-to-all-start = ((s32[8,1,128]{2,1,0:T(1,128)}), s32[8,1,128]{2,1,0:T(1,128)S(1)}, u32[]{:S(2)}, u32[]{:S(2)}) async-start(s32[8,1,128]{2,1,0:T(1,128)} %broadcast_in_dim.21), calls=%async_computation | async-start | bytes 8192 | tf_op jit(solution)/shard_map/all_to_all | solution.py:561
  10.1 1.1 %collective-permute-start = (s32[65]{0:T(128)S(1)}, s32[65]{0:T(128)S(1)}, u32[]{:S(2)}, u32[]{:S(2)}) collective-permute-start(s32[65]{0:T(128)S(1)} %pad_add_fusion.1.meta_a), channel_id=1, source_target_pairs={{0,2},{2,0},{1,3},{3,1},{4,6},{6,4},{5,7},{7,5},{8,10},{10,8},{9,1... | collective-permute-start | bytes 788 | tf_op jit(solution)/shard_map/ppermute | solution.py:560
  16.8 2.0 %collective-permute-start.2 = (bf16[8,256,128]{2,1,0:T(8,128)(2,1)S(1)}, bf16[8,256,128]{2,1,0:T(8,128)(2,1)S(1)}, u32[]{:S(2)}, u32[]{:S(2)}) collective-permute-start(bf16[8,256,128]{2,1,0:T(8,128)(2,1)S(1)} %pick.1.picked), channel_id=1, source_target_pairs={{0,2},{2,0},{1,3},{3,1},{4,6},{6,4},{5,7},{7,5},{8,10},{10,8},{9,1... | collective-permute-start | bytes 1572872 | tf_op jit(solution)/shard_map/ppermute | solution.py:573
  16.9 3.4 %collective-permute-start.1 = (s32[8,128]{1,0:T(8,128)S(1)}, s32[8,128]{1,0:T(8,128)S(1)}, u32[]{:S(2)}, u32[]{:S(2)}) collective-permute-start(s32[8,128]{1,0:T(8,128)S(1)} %bitcast.16), channel_id=1, source_target_pairs={{0,2},{2,0},{1,3},{3,1},{4,6},{6,4},{5,7},{7,5},{8,10},{10,8},{9,1... | collective-permute-start | bytes 12296 | tf_op jit(solution)/shard_map/ppermute | solution.py:574
  25.3 14.3 %all-to-all-start.1 = ((bf16[8,256,128]{2,1,0:T(8,128)(2,1)}), bf16[8,256,128]{2,1,0:T(8,128)(2,1)S(1)}, u32[]{:S(2)}, u32[]{:S(2)}) async-start(bf16[8,256,128]{2,1,0:T(8,128)(2,1)} %pack.1.start.previous), calls=%async_computation.1 | async-start | bytes 1048576 | tf_op jit(solution)/shard_map/all_to_all | solution.py:602
  28.8 1.4 %collective-permute-start.3 = (s32[2048]{0:T(1024)}, s32[2048]{0:T(1024)S(1)}, u32[]{:S(2)}, u32[]{:S(2)}) collective-permute-start(s32[2048]{0:T(1024)} %get-tuple-element.26), channel_id=1, source_target_pairs={{0,2},{2,0},{1,3},{3,1},{4,6},{6,4},{5,7},{7,5},{8,10},{10,8},{9,1... | collective-permute-start | bytes 24584 | tf_op jit(solution)/shard_map/ppermute | solution.py:606
  30.2 0.7 copy-start
  60.5 16.9 %all-to-all-start.3 = ((bf16[8,256,128]{2,1,0:T(8,128)(2,1)}), bf16[8,256,128]{2,1,0:T(8,128)(2,1)S(1)}, u32[]{:S(2)}, u32[]{:S(2)}) async-start(bf16[8,256,128]{2,1,0:T(8,128)(2,1)} %sent.3), calls=%async_computation.3 | async-start | bytes 1048576 | tf_op jit(solution)/shard_map/all_to_all | solution.py:718
  64.2 1.9 %collective-permute-start.5 = (bf16[8,256,128]{2,1,0:T(8,128)(2,1)S(1)}, bf16[8,256,128]{2,1,0:T(8,128)(2,1)S(1)}, u32[]{:S(2)}, u32[]{:S(2)}) collective-permute-start(bf16[8,256,128]{2,1,0:T(8,128)(2,1)S(1)} %all-to-all-done.1.pieces.q1), channel_id=1, source_target_pairs={{0,2},{2,0},{1,3},{3,1},{4,6},{6,4},{5,7},{7,5},{8,10},{10,8},{9,1... | collective-permute-start | bytes 1572872 | tf_op jit(solution)/shard_map/ppermute | solution.py:715
  64.2 2.7 %collective-permute-start.6 = (bf16[8,256,128]{2,1,0:T(8,128)(2,1)S(1)}, bf16[8,256,128]{2,1,0:T(8,128)(2,1)S(1)}, u32[]{:S(2)}, u32[]{:S(2)}) collective-permute-start(bf16[8,256,128]{2,1,0:T(8,128)(2,1)S(1)} %all_to_all.24.pieces.q2), channel_id=1, source_target_pairs={{0,2},{2,0},{1,3},{3,1},{4,6},{6,4},{5,7},{7,5},{8,10},{10,8},{9,1... | collective-permute-start | bytes 1572872 | tf_op jit(solution)/shard_map/ppermute | solution.py:716
  77.4 2.0 %collective-permute-start.7 = (bf16[8,256,128]{2,1,0:T(8,128)(2,1)S(1)}, bf16[8,256,128]{2,1,0:T(8,128)(2,1)S(1)}, u32[]{:S(2)}, u32[]{:S(2)}) collective-permute-start(bf16[8,256,128]{2,1,0:T(8,128)(2,1)S(1)} %all-to-all-done.3.mine), channel_id=1, source_target_pairs={{0,2},{2,0},{1,3},{3,1},{4,6},{6,4},{5,7},{7,5},{8,10},{10,8},{9,1... | collective-permute-start | bytes 1572872 | tf_op jit(solution)/shard_map/ppermute | solution.py:719
where the time goes:
time: 83.9 us; the launch traced here: 83.4 us
  Pallas kernels  28.3 us (34%)
  waiting for transfers between devices  20.4 us (24%)
  starting transfers between devices  15.8 us (19%)
  blocking collectives  15.1 us (18%)
  other arithmetic  1.61 us (2%)
  local copies, waits for them, and re-layouts  1.37 us (2%)
    pallas_call x9, Pallas kernels, call(): pl.pallas_call(kernel, out_shape=[space(shape, dtype) for shape, dtype, s...  28.3 us
    all_to_all x1, blocking collectives, on_pair(): q2 = exchange(first_sent)  15.1 us
    all_to_all x1, waiting for transfers between devices, on_pair(): q1 = exchange(after(packed, own_list))  7.4 us
    all_to_all x1, starting transfers between devices, on_pair(): exchange(jnp.broadcast_to(needed, (n_row, LANES)))  6.8 us
    all_to_all x1, waiting for transfers between devices, on_pair(): exchange(jnp.broadcast_to(needed, (n_row, LANES)))  3.86 us
    all_to_all x1, starting transfers between devices, on_pair(): q3 = after(exchange(second_sent), base)  3.69 us
    all_to_all x1, starting transfers between devices, on_pair(): q1 = exchange(after(packed, own_list))  3.51 us
    all_to_all x1, waiting for transfers between devices, on_pair(): q3 = after(exchange(second_sent), base)  3.36 us
  transfers between devices with their start and end apart: 11, of which 8 were waited for; matrix products, arithmetic and copies ran while one was open for 3% of the time, Pallas kernels for 22%

commit v1 on v0

--- a/solution.py
+++ b/solution.py
@@ -65,8 +65,12 @@
     place,
     wanted_a,
     wanted_b,
-    meta_a,
-    meta_b,
+    rows_a,
+    cols_a,
+    used_a,
+    rows_b,
+    cols_b,
+    used_b,
     own,
     other,
     out,
@@ -75,20 +79,19 @@
     seen,
     sems,
 ):
-    slot_count = (meta_a.shape[0] - 1) // 2
+    slot_count = rows_a.shape[0]
 
     def put(at, *values):
         for i, value in enumerate(values):
             out[at + i] = value
 
-    def scan(tile, meta):
-        used = meta[2 * slot_count]
+    def scan(tile, rows, cols, used):
 
         def step(s, carry):
             ends, sent, load = carry
-            row = meta[s]
-            piece = meta[slot_count + s] // piece_blocks
-            live = s < used
+            row = rows[s]
+            piece = cols[s] // piece_blocks
+            live = s < used[0]
             half = row // piece_blocks
             local = row - half * piece_blocks
             lower = half == 0
@@ -172,8 +175,8 @@
                 number = count[row]
                 asked[row * n_row + number] = k
                 count[row] = number + 1
-        scan(0, meta_a)
-        scan(1, meta_b)
+        scan(0, rows_a, cols_a, used_a)
+        scan(1, rows_b, cols_b, used_b)
         for core in range(2):
             mark(core)
         copies = [
@@ -370,16 +373,14 @@
 
     @pl.when(half == 0)
     def _():
-        @pl.loop(0, n_row)
-        def _(p):
+        for p in range(n_row):
             one, two = mine[p], other[p]
             vec[0, p, :, at : at + width] = jnp.concatenate([one[:, :middle], two[:, middle:]], axis=1)
             vec[1, p, :, at : at + width] = jnp.concatenate([one[:, middle:], two[:, :middle]], axis=1)
 
     @pl.when(half != 0)
     def _():
-        @pl.loop(0, n_row)
-        def _(p):
+        for p in range(n_row):
             one, two = mine[p], other[p]
             vec[0, p, :, at : at + width] = jnp.concatenate([two[:, middle:], one[:, :middle]], axis=1)
             vec[1, p, :, at : at + width] = jnp.concatenate([two[:, :middle], one[:, middle:]], axis=1)
@@ -556,9 +557,7 @@
     exchange = functools.partial(
         lax.all_to_all, axis_name="row", split_axis=0, concat_axis=0, tiled=True
     )
-    meta = jnp.concatenate([slot_rows, slot_cols, used])
-    meta_other = across(meta)
-    wanted = after(exchange(jnp.broadcast_to(needed, (n_row, LANES))), meta_other, place)
+    wanted = exchange(jnp.broadcast_to(needed, (n_row, LANES)))
     sent_shape = (n_row, block_size, width)
     (sent,) = call(
         functools.partial(pick_kernel, n_row, block_size),
@@ -572,6 +571,8 @@
     tile_other = across(tile)
     sent_other = across(sent)
     wanted_other = across(after(wanted, sent))
+    slots = (slot_rows, slot_cols, used)
+    slots_other = [across(after(array, sent)) for array in slots]
     packed = call(
         pack_kernel,
         [(sent_shape, jnp.bfloat16, HBM)],
@@ -587,8 +588,8 @@
     own_list, other_list = call(
         functools.partial(plan_kernel, n_row, piece_blocks, lay),
         [(*list_shape, HBM)] * 2,
-        (place, wanted, after(wanted_other, packed), meta, meta_other),
-        (SCALARS,) * 5,
+        (place, wanted, after(wanted_other, packed), *slots, *slots_other),
+        (SCALARS,) * 9,
         [
             SMEM((2 * lay.size,), jnp.int32),
             SMEM((2 * piece_blocks,), jnp.int32),

time: 83.9 us -> 85.2 us (1.015)
  blocking collectives: 15.1 us -> 30.2 us
  starting transfers between devices: 15.8 us -> 9.58 us
  waiting for transfers between devices: 20.4 us -> 16.3 us
  Pallas kernels: 28.3 us -> 26.6 us
    all_to_all x0 -> x1, blocking collectives: none -> 13.1 us  [on_pair(): wanted = exchange(jnp.broadcast_to(needed, (n_row, LANES)))]
    all_to_all x1 -> x0, starting transfers between devices: 6.8 us -> none  [on_pair(): exchange(jnp.broadcast_to(needed, (n_row, LANES)))]
    all_to_all x1 -> x0, waiting for transfers between devices: 3.86 us -> none  [on_pair(): exchange(jnp.broadcast_to(needed, (n_row, LANES)))]
    all_to_all x1, blocking collectives: 15.1 us -> 17.1 us  [on_pair(): q2 = exchange(first_sent)]
    pallas_call x9, Pallas kernels: 28.3 us -> 26.6 us  [call(): pl.pallas_call(kernel, out_shape=[space(shape, dtype) for shape, dtype, s...]
    all_to_all x1, waiting for transfers between devices: 3.36 us -> 4.69 us  [on_pair(): q3 = after(exchange(second_sent), base)]
    ppermute x1, waiting for transfers between devices: 1.4 us -> 0.1 us  [on_pair(): sent_other = across(sent)]
  transfers between devices with their start and end apart: 11 -> 12, of which waited for: 8 -> 6; matrix products, arithmetic and copies ran while one was open for 3% -> 1% of each run, Pallas kernels for 22% -> 22%
where the time goes in v1:
time: 85.2 us
  blocking collectives  30.2 us (35%)
  Pallas kernels  26.6 us (31%)
  waiting for transfers between devices  16.3 us (19%)
  starting transfers between devices  9.58 us (11%)
  other arithmetic  0.86 us (1%)
    pallas_call x9, Pallas kernels, call(): pl.pallas_call(kernel, out_shape=[space(shape, dtype) for shape, dtype, s...  26.6 us
    all_to_all x1, blocking collectives, on_pair(): q2 = exchange(first_sent)  17.1 us
    all_to_all x1, blocking collectives, on_pair(): wanted = exchange(jnp.broadcast_to(needed, (n_row, LANES)))  13.1 us
    all_to_all x1, waiting for transfers between devices, on_pair(): q1 = exchange(after(packed, own_list))  8 us
    all_to_all x1, waiting for transfers between devices, on_pair(): q3 = after(exchange(second_sent), base)  4.69 us
    all_to_all x1, starting transfers between devices, on_pair(): q3 = after(exchange(second_sent), base)  3.77 us
    all_to_all x1, starting transfers between devices, on_pair(): q1 = exchange(after(packed, own_list))  3.51 us
  transfers between devices with their start and end apart: 12, of which 6 were waited for; matrix products, arithmetic and copies ran while one was open for 1% of the time, Pallas kernels for 22%

profile of v1, /device:TPU:0, one launch (start us, length us, event | category | flops | bytes accessed | tf_op | source)
XLA Modules:
  0.0 85.2 jit_solution(17536056403988877053)
XLA Ops:
  0.0 0.5 collective-permute-start.6
  0.5 0.7 and_select_fusion.1
  1.3 13.1 %all_to_all.23 = s32[8,1,128]{2,1,0:T(1,128)S(1)} all-to-all(s32[8,1,128]{2,1,0:T(1,128)S(1)} %broadcast_in_dim.21), channel_id=1, replica_groups=mesh['row'=8,'col'=2,'vec'=2] {'row'}, dimensions={0} | all-to-all | bytes 8192 | tf_op jit(solution)/shard_map/all_to_all | solution.py:560
  14.4 1.7 %pick.1.picked = bf16[8,256,128]{2,1,0:T(8,128)(2,1)S(1)} custom-call(s32[8,128]{1,0:T(8,128)S(1)} %bitcast.15, bf16[8192,128]{1,0:T(8,128)(2,1)} %vectors.3), custom_call_target="tpu_custom_call" | custom-call | tf_op jit(solution)/shard_map/pick/pallas_call | solution.py:516
  16.3 0.5 collective-permute-start
  17.6 0.4 collective-permute-start.3
  18.3 1.5 %pack.1.start.previous = bf16[8,256,128]{2,1,0:T(8,128)(2,1)} custom-call(s32[2]{0:T(128)S(1)} %pad_add_fusion.place, bf16[8,256,128]{2,1,0:T(8,128)(2,1)S(1)} %pick.1.picked, bf16[8,256,128]{2,1,0:T(8,128)(2,1)S(1)} %collective-permute-done.1.picked_b), custom_call_target="tpu_custom_call" | custom-call | tf_op jit(solution)/shard_map/pack/pallas_call | solution.py:516
  19.8 5.3 %plan.1 = (s32[2048]{0:T(1024)}, s32[2048]{0:T(1024)}) custom-call(s32[2]{0:T(128)S(1)} %pad_add_fusion.place, s32[8,128]{1,0:T(8,128)S(1)} %bitcast.17, s32[8,128]{1,0:T(8,128)S(1)} %collective-permute-done.wanted_b, s32[32]{0:T(128)S(1)} %bitcast.21, s32[32]{0:T(128)S(1)} %bitcast.19, s32[1]{0:T(128)} %bitcast.14.used_a, ...), custom_call_target="tpu_custom_call" | custom-call | tf_op jit(solution)/shard_map/plan/pallas_call | solution.py:516
  25.1 3.5 %all-to-all-start.1 = ((bf16[8,256,128]{2,1,0:T(8,128)(2,1)}), bf16[8,256,128]{2,1,0:T(8,128)(2,1)S(1)}, u32[]{:S(2)}, u32[]{:S(2)}) async-start(bf16[8,256,128]{2,1,0:T(8,128)(2,1)} %pack.1.start.previous), calls=%async_computation.1 | async-start | bytes 1048576 | tf_op jit(solution)/shard_map/all_to_all | solution.py:603
  28.7 1.4 %collective-permute-done.5.handed = s32[2048]{0:T(1024)S(1)} collective-permute-done((s32[2048]{0:T(1024)}, s32[2048]{0:T(1024)S(1)}, u32[]{:S(2)}, u32[]{:S(2)}) %collective-permute-start.5) | collective-permute-done | bytes 8224 | tf_op jit(solution)/shard_map/ppermute | solution.py:607
  30.1 0.7 copy-done
  30.8 1.2 %settle.1.plan = s32[2048]{0:T(1024)S(4)} custom-call(s32[2]{0:T(128)S(1)} %pad_add_fusion.place, s32[2048]{0:T(1024)S(1)} %copy-done, s32[2048]{0:T(1024)S(1)} %collective-permute-done.5.handed), custom_call_target="tpu_custom_call" | custom-call | tf_op jit(solution)/shard_map/settle/pallas_call | solution.py:516
  32.0 8.0 %all-to-all-done.1.pieces.q1 = bf16[8,256,128]{2,1,0:T(8,128)(2,1)S(1)} async-done(((bf16[8,256,128]{2,1,0:T(8,128)(2,1)}), bf16[8,256,128]{2,1,0:T(8,128)(2,1)S(1)}, u32[]{:S(2)}, u32[]{:S(2)}) %all-to-all-start.1) | async-done | bytes 524320 | tf_op jit(solution)/shard_map/all_to_all | solution.py:603
  40.0 2.5 %sent.2 = (bf16[8,256,128]{2,1,0:T(8,128)(2,1)S(1)}, bf16[66,256,256]{2,1,0:T(8,128)(2,1)S(1)}) custom-call(s32[2048]{0:T(1024)S(4)} %settle.1.plan, bf16[32,256,256]{2,1,0:T(8,128)(2,1)} %bitcast.23, bf16[32,256,256]{2,1,0:T(8,128)(2,1)} %collective-permute-done.6.tile_b, bf16[8,256,128]{2,1,0:T(8,128)(2,1)S(1)} %all-to-all-done.1.pieces.q1, ...), custom_call_target="tpu_custom_call" | custom-call | flops 134217728 | bytes 2621440 | tf_op jit(solution)/shard_map/sent/pallas_call | solution.py:516
  42.5 17.1 %all_to_all.24.pieces.q2 = bf16[8,256,128]{2,1,0:T(8,128)(2,1)S(1)} all-to-all(bf16[8,256,128]{2,1,0:T(8,128)(2,1)S(1)} %get-tuple-element.34.current), channel_id=1, replica_groups=mesh['row'=8,'col'=2,'vec'=2] {'row'}, dimensions={0} | all-to-all | bytes 1048576 | tf_op jit(solution)/shard_map/all_to_all | solution.py:714
  59.6 2.1 %sent.3 = bf16[8,256,128]{2,1,0:T(8,128)(2,1)} custom-call(s32[2048]{0:T(1024)S(4)} %settle.1.plan, bf16[66,256,256]{2,1,0:T(8,128)(2,1)S(1)} %get-tuple-element.33.blocks, bf16[8,256,128]{2,1,0:T(8,128)(2,1)S(1)} %all_to_all.24.pieces.q2, bf16[8,256,128]{2,1,0:T(8,128)(2,1)S(1)} %get-tuple-element.34.current, bf16[8,256,128]{2,1,0:T(8,128)(2,1)} %pack.1.start.previous), custom_call_target="tpu_custom_call" | custom-call | flops 134217728 | bytes 2621440 | tf_op jit(solution)/shard_map/sent/pallas_call | solution.py:516
  61.7 3.8 %all-to-all-start.3 = ((bf16[8,256,128]{2,1,0:T(8,128)(2,1)}), bf16[8,256,128]{2,1,0:T(8,128)(2,1)S(1)}, u32[]{:S(2)}, u32[]{:S(2)}) async-start(bf16[8,256,128]{2,1,0:T(8,128)(2,1)} %sent.3), calls=%async_computation.3 | async-start | bytes 1048576 | tf_op jit(solution)/shard_map/all_to_all | solution.py:719
  65.5 0.5 collective-permute-start.8
  66.0 1.4 %collective-permute-done.7.q1_other = bf16[8,256,128]{2,1,0:T(8,128)(2,1)S(1)} collective-permute-done((bf16[8,256,128]{2,1,0:T(8,128)(2,1)S(1)}, bf16[8,256,128]{2,1,0:T(8,128)(2,1)S(1)}, u32[]{:S(2)}, u32[]{:S(2)}) %collective-permute-start.7) | collective-permute-done | bytes 524320 | tf_op jit(solution)/shard_map/ppermute | solution.py:716
  67.4 0.7 collective-permute-done.8.q2_other
  68.1 6.7 %early.1.array = bf16[32,256,128]{2,1,0:T(8,128)(2,1)} custom-call(s32[2048]{0:T(1024)S(4)} %settle.1.plan, bf16[32,256,256]{2,1,0:T(8,128)(2,1)} %bitcast.24, bf16[32,256,256]{2,1,0:T(8,128)(2,1)} %collective-permute-done.6.tile_b, bf16[8,256,128]{2,1,0:T(8,128)(2,1)S(1)} %all-to-all-done.1.pieces.q1, ...), custom_call_target="tpu_custom_call" | custom-call | flops 1073741824 | bytes 20971520 | tf_op jit(solution)/shard_map/early/pallas_call | solution.py:516
  74.8 4.7 %all-to-all-done.3.mine = bf16[8,256,128]{2,1,0:T(8,128)(2,1)S(1)} async-done(((bf16[8,256,128]{2,1,0:T(8,128)(2,1)}), bf16[8,256,128]{2,1,0:T(8,128)(2,1)S(1)}, u32[]{:S(2)}, u32[]{:S(2)}) %all-to-all-start.3) | async-done | bytes 524320 | tf_op jit(solution)/shard_map/all_to_all | solution.py:719
  79.5 2.0 %load.1 = (bf16[36,256,256]{2,1,0:T(8,128)(2,1)S(1)}, bf16[32,256,128]{2,1,0:T(8,128)(2,1)S(1)}) custom-call(s32[2048]{0:T(1024)S(4)} %settle.1.plan, bf16[32,256,256]{2,1,0:T(8,128)(2,1)} %bitcast.25, bf16[32,256,128]{2,1,0:T(8,128)(2,1)} %early.1.array), custom_call_target="tpu_custom_call" | custom-call | tf_op jit(solution)/shard_map/load/pallas_call | solution.py:516
  81.5 3.7 %last.1 = bf16[32,256,128]{2,1,0:T(8,128)(2,1)} custom-call(s32[2048]{0:T(1024)S(4)} %settle.1.plan, bf16[36,256,256]{2,1,0:T(8,128)(2,1)S(1)} %get-tuple-element.39.blocks, bf16[32,256,256]{2,1,0:T(8,128)(2,1)} %collective-permute-done.6.tile_b, bf16[8,256,128]{2,1,0:T(8,128)(2,1)S(1)} %all-to-all-done.3.mine, ...), custom_call_target="tpu_custom_call" | custom-call | flops 536870912 | bytes 10485760 | tf_op jit(solution)/shard_map/last/pallas_call | solution.py:516
  (21 shorter events, 0.8 us)
Async XLA Ops:
  0.0 19.8 %copy-start.1 = (s32[1,1,32]{2,1,0:T(1,128)S(1)}, s32[1,1,32]{2,1,0:T(1,128)}, u32[]{:S(2)}) copy-start(s32[1,1,32]{2,1,0:T(1,128)} %param.8) | copy-start | bytes 388
  0.0 19.8 %copy-start.2 = (s32[1,1,32]{2,1,0:T(1,128)S(1)}, s32[1,1,32]{2,1,0:T(1,128)}, u32[]{:S(2)}) copy-start(s32[1,1,32]{2,1,0:T(1,128)} %param.7) | copy-start | bytes 388
  0.0 40.0 %collective-permute-start.6 = (bf16[32,256,256]{2,1,0:T(8,128)(2,1)}, bf16[32,256,256]{2,1,0:T(8,128)(2,1)}, u32[]{:S(2)}, u32[]{:S(2)}) collective-permute-start(bf16[32,256,256]{2,1,0:T(8,128)(2,1)} %bitcast.22), channel_id=1, source_target_pairs={{0,2},{2,0},{1,3},{3,1},{4,6},{6,4},{5,7},{7,5},{8,10},{10,8},{9,1... | collective-permute-start | bytes 12582920 | tf_op jit(solution)/shard_map/ppermute | solution.py:571
  16.2 2.0 %collective-permute-start.1 = (bf16[8,256,128]{2,1,0:T(8,128)(2,1)S(1)}, bf16[8,256,128]{2,1,0:T(8,128)(2,1)S(1)}, u32[]{:S(2)}, u32[]{:S(2)}) collective-permute-start(bf16[8,256,128]{2,1,0:T(8,128)(2,1)S(1)} %pick.1.picked), channel_id=1, source_target_pairs={{0,2},{2,0},{1,3},{3,1},{4,6},{6,4},{5,7},{7,5},{8,10},{10,8},{9,1... | collective-permute-start | bytes 1572872 | tf_op jit(solution)/shard_map/ppermute | solution.py:572
  16.3 3.5 %collective-permute-start = (s32[8,128]{1,0:T(8,128)S(1)}, s32[8,128]{1,0:T(8,128)S(1)}, u32[]{:S(2)}, u32[]{:S(2)}) collective-permute-start(s32[8,128]{1,0:T(8,128)S(1)} %bitcast.16), channel_id=1, source_target_pairs={{0,2},{2,0},{1,3},{3,1},{4,6},{6,4},{5,7},{7,5},{8,10},{10,8},{9,1... | collective-permute-start | bytes 12296 | tf_op jit(solution)/shard_map/ppermute | solution.py:573
  17.5 2.3 %collective-permute-start.2 = (s32[32]{0:T(128)}, s32[32]{0:T(128)S(1)}, u32[]{:S(2)}, u32[]{:S(2)}) collective-permute-start(s32[32]{0:T(128)} %bitcast.20), channel_id=1, source_target_pairs={{0,2},{2,0},{1,3},{3,1},{4,6},{6,4},{5,7},{7,5},{8,10},{10,8},{9,1... | collective-permute-start | bytes 392 | tf_op jit(solution)/shard_map/ppermute | solution.py:575
  17.6 2.2 %collective-permute-start.3 = (s32[32]{0:T(128)}, s32[32]{0:T(128)S(1)}, u32[]{:S(2)}, u32[]{:S(2)}) collective-permute-start(s32[32]{0:T(128)} %bitcast.18), channel_id=1, source_target_pairs={{0,2},{2,0},{1,3},{3,1},{4,6},{6,4},{5,7},{7,5},{8,10},{10,8},{9,1... | collective-permute-start | bytes 392 | tf_op jit(solution)/shard_map/ppermute | solution.py:575
  18.2 1.6 %collective-permute-start.4 = (s32[1]{0:T(128)}, s32[1]{0:T(128)}, u32[]{:S(2)}, u32[]{:S(2)}) collective-permute-start(s32[1]{0:T(128)} %bitcast.5), channel_id=1, source_target_pairs={{0,2},{2,0},{1,3},{3,1},{4,6},{6,4},{5,7},{7,5},{8,10},{10,8},{9,1... | collective-permute-start | bytes 20 | tf_op jit(solution)/shard_map/ppermute | solution.py:575
  25.1 14.9 %all-to-all-start.1 = ((bf16[8,256,128]{2,1,0:T(8,128)(2,1)}), bf16[8,256,128]{2,1,0:T(8,128)(2,1)S(1)}, u32[]{:S(2)}, u32[]{:S(2)}) async-start(bf16[8,256,128]{2,1,0:T(8,128)(2,1)} %pack.1.start.previous), calls=%async_computation.1 | async-start | bytes 1048576 | tf_op jit(solution)/shard_map/all_to_all | solution.py:603
  28.6 1.4 %collective-permute-start.5 = (s32[2048]{0:T(1024)}, s32[2048]{0:T(1024)S(1)}, u32[]{:S(2)}, u32[]{:S(2)}) collective-permute-start(s32[2048]{0:T(1024)} %get-tuple-element.30), channel_id=1, source_target_pairs={{0,2},{2,0},{1,3},{3,1},{4,6},{6,4},{5,7},{7,5},{8,10},{10,8},{9,1... | collective-permute-start | bytes 24584 | tf_op jit(solution)/shard_map/ppermute | solution.py:607
  30.1 0.7 copy-start
  61.7 17.8 %all-to-all-start.3 = ((bf16[8,256,128]{2,1,0:T(8,128)(2,1)}), bf16[8,256,128]{2,1,0:T(8,128)(2,1)S(1)}, u32[]{:S(2)}, u32[]{:S(2)}) async-start(bf16[8,256,128]{2,1,0:T(8,128)(2,1)} %sent.3), calls=%async_computation.3 | async-start | bytes 1048576 | tf_op jit(solution)/shard_map/all_to_all | solution.py:719
  65.5 1.9 %collective-permute-start.7 = (bf16[8,256,128]{2,1,0:T(8,128)(2,1)S(1)}, bf16[8,256,128]{2,1,0:T(8,128)(2,1)S(1)}, u32[]{:S(2)}, u32[]{:S(2)}) collective-permute-start(bf16[8,256,128]{2,1,0:T(8,128)(2,1)S(1)} %all-to-all-done.1.pieces.q1), channel_id=1, source_target_pairs={{0,2},{2,0},{1,3},{3,1},{4,6},{6,4},{5,7},{7,5},{8,10},{10,8},{9,1... | collective-permute-start | bytes 1572872 | tf_op jit(solution)/shard_map/ppermute | solution.py:716
  65.5 2.7 %collective-permute-start.8 = (bf16[8,256,128]{2,1,0:T(8,128)(2,1)S(1)}, bf16[8,256,128]{2,1,0:T(8,128)(2,1)S(1)}, u32[]{:S(2)}, u32[]{:S(2)}) collective-permute-start(bf16[8,256,128]{2,1,0:T(8,128)(2,1)S(1)} %all_to_all.24.pieces.q2), channel_id=1, source_target_pairs={{0,2},{2,0},{1,3},{3,1},{4,6},{6,4},{5,7},{7,5},{8,10},{10,8},{9,1... | collective-permute-start | bytes 1572872 | tf_op jit(solution)/shard_map/ppermute | solution.py:717
  79.5 2.0 %collective-permute-start.9 = (bf16[8,256,128]{2,1,0:T(8,128)(2,1)S(1)}, bf16[8,256,128]{2,1,0:T(8,128)(2,1)S(1)}, u32[]{:S(2)}, u32[]{:S(2)}) collective-permute-start(bf16[8,256,128]{2,1,0:T(8,128)(2,1)S(1)} %all-to-all-done.3.mine), channel_id=1, source_target_pairs={{0,2},{2,0},{1,3},{3,1},{4,6},{6,4},{5,7},{7,5},{8,10},{10,8},{9,1... | collective-permute-start | bytes 1572872 | tf_op jit(solution)/shard_map/ppermute | solution.py:720

commit v2 on v1

--- a/solution.py
+++ b/solution.py
@@ -74,7 +74,6 @@
     own,
     other,
     out,
-    count,
     asked,
     seen,
     sems,
@@ -99,7 +98,9 @@
             at = HEAD + STRIDE * (part * lay.slots + jnp.where(lower, ends[0], ends[1]))
             base = half * lay.size
             put(base + at, s, local, piece)
-            found = jnp.where(live, count[row], 0)
+            sought = jnp.where(live, local, -1)
+            hits = [(asked[half * n_row + k] == sought).astype(jnp.int32) for k in range(n_row)]
+            found = sum(hits)
 
             @pl.when(found > 0)
             def _():
@@ -109,15 +110,16 @@
                     first = core * lay.size
                     out[first + lay.load_at + mine * lay.loads + load] = s
 
-                    @pl.loop(0, found)
-                    def _(j):
+                    place = sent
+                    for k in range(n_row):
                         put(
-                            first + lay.sent_at + STRIDE * (mine * lay.sends + sent + j),
+                            first + lay.sent_at + STRIDE * (mine * lay.sends + place),
                             mine * lay.loads + load,
-                            2 * asked[row * n_row + j] + side,
+                            2 * k + side,
                             piece,
-                            jnp.where(j == 0, FIRST, 0),
+                            jnp.where(place == sent, FIRST, 0),
                         )
+                        place = place + hits[k]
 
             one = live.astype(jnp.int32)
             ends = (ends[0] + jnp.where(lower, one, 0), ends[1] + jnp.where(lower, 0, one))
@@ -167,14 +169,9 @@
 
     @pl.when(place[1] == 0)
     def _():
-        for row in range(2 * piece_blocks):
-            count[row] = 0
         for half, wanted in enumerate((wanted_a, wanted_b)):
             for k in range(n_row):
-                row = half * piece_blocks + wanted[k, 0]
-                number = count[row]
-                asked[row * n_row + number] = k
-                count[row] = number + 1
+                asked[half * n_row + k] = wanted[k, 0]
         scan(0, rows_a, cols_a, used_a)
         scan(1, rows_b, cols_b, used_b)
         for core in range(2):
@@ -592,8 +589,7 @@
         (SCALARS,) * 9,
         [
             SMEM((2 * lay.size,), jnp.int32),
-            SMEM((2 * piece_blocks,), jnp.int32),
-            SMEM((2 * piece_blocks * n_row,), jnp.int32),
+            SMEM((2 * n_row,), jnp.int32),
             SMEM((piece_blocks + 1,), jnp.int32),
             DMA((2,)),
         ],

time: 85.2 us -> 82.6 us (0.969)
  Pallas kernels: 26.6 us -> 33.3 us
  waiting for transfers between devices: 16.3 us -> 10.5 us
  blocking collectives: 30.2 us -> 26.3 us
    pallas_call x9, Pallas kernels: 26.6 us -> 33.3 us  [call(): pl.pallas_call(kernel, out_shape=[space(shape, dtype) for shape, dtype, s...]
    all_to_all x1, waiting for transfers between devices: 4.69 us -> 0.01 us  [on_pair(): q3 = after(exchange(second_sent), base)]
    all_to_all x1, blocking collectives: 17.1 us -> 13.2 us  [on_pair(): q2 = exchange(first_sent)]
    all_to_all x1, waiting for transfers between devices: 8 us -> 6.82 us  [on_pair(): q1 = exchange(after(packed, own_list))]
  transfers between devices with their start and end apart: 12 -> 12, of which waited for: 6 -> 5; matrix products, arithmetic and copies ran while one was open for 1% -> 1% of each run, Pallas kernels for 22% -> 28%
where the time goes in v2:
time: 82.6 us; the launch traced here: 82.1 us
  Pallas kernels  33.3 us (40%)
  blocking collectives  26.3 us (32%)
  waiting for transfers between devices  10.5 us (13%)
  starting transfers between devices  9.58 us (12%)
  other arithmetic  0.86 us (1%)
  between operations  0.84 us (1%)
    pallas_call x9, Pallas kernels, call(): pl.pallas_call(kernel, out_shape=[space(shape, dtype) for shape, dtype, s...  33.3 us
    all_to_all x1, blocking collectives, on_pair(): q2 = exchange(first_sent)  13.2 us
    all_to_all x1, blocking collectives, on_pair(): wanted = exchange(jnp.broadcast_to(needed, (n_row, LANES)))  13.1 us
    all_to_all x1, waiting for transfers between devices, on_pair(): q1 = exchange(after(packed, own_list))  6.82 us
    all_to_all x1, starting transfers between devices, on_pair(): q1 = exchange(after(packed, own_list))  3.51 us
    all_to_all x1, starting transfers between devices, on_pair(): q3 = after(exchange(second_sent), base)  3.5 us
  transfers between devices with their start and end apart: 12, of which 5 were waited for; matrix products, arithmetic and copies ran while one was open for 1% of the time, Pallas kernels for 28%

profile of v2, /device:TPU:0, one launch (start us, length us, event | category | flops | bytes accessed | tf_op | source)
XLA Modules:
  0.0 82.1 jit_solution(7256496001307691370)
XLA Ops:
  0.0 0.5 collective-permute-start.6
  0.5 0.7 and_select_fusion.1
  1.3 13.1 %all_to_all.23 = s32[8,1,128]{2,1,0:T(1,128)S(1)} all-to-all(s32[8,1,128]{2,1,0:T(1,128)S(1)} %broadcast_in_dim.21), channel_id=1, replica_groups=mesh['row'=8,'col'=2,'vec'=2] {'row'}, dimensions={0} | all-to-all | bytes 8192 | tf_op jit(solution)/shard_map/all_to_all | solution.py:557
  14.4 1.7 %pick.1.picked = bf16[8,256,128]{2,1,0:T(8,128)(2,1)S(1)} custom-call(s32[8,128]{1,0:T(8,128)S(1)} %bitcast.15, bf16[8192,128]{1,0:T(8,128)(2,1)} %vectors.3), custom_call_target="tpu_custom_call" | custom-call | tf_op jit(solution)/shard_map/pick/pallas_call | solution.py:513
  16.3 0.5 collective-permute-start
  17.6 0.4 collective-permute-start.3
  18.3 1.5 %pack.1.start.previous = bf16[8,256,128]{2,1,0:T(8,128)(2,1)} custom-call(s32[2]{0:T(128)S(1)} %pad_add_fusion.place, bf16[8,256,128]{2,1,0:T(8,128)(2,1)S(1)} %pick.1.picked, bf16[8,256,128]{2,1,0:T(8,128)(2,1)S(1)} %collective-permute-done.1.picked_b), custom_call_target="tpu_custom_call" | custom-call | tf_op jit(solution)/shard_map/pack/pallas_call | solution.py:513
  19.8 7.4 %plan.1 = (s32[2048]{0:T(1024)}, s32[2048]{0:T(1024)}) custom-call(s32[2]{0:T(128)S(1)} %pad_add_fusion.place, s32[8,128]{1,0:T(8,128)S(1)} %bitcast.17, s32[8,128]{1,0:T(8,128)S(1)} %collective-permute-done.wanted_b, s32[32]{0:T(128)S(1)} %bitcast.21, s32[32]{0:T(128)S(1)} %bitcast.19, s32[1]{0:T(128)} %bitcast.14.used_a, ...), custom_call_target="tpu_custom_call" | custom-call | tf_op jit(solution)/shard_map/plan/pallas_call | solution.py:513
  27.3 3.5 %all-to-all-start.1 = ((bf16[8,256,128]{2,1,0:T(8,128)(2,1)}), bf16[8,256,128]{2,1,0:T(8,128)(2,1)S(1)}, u32[]{:S(2)}, u32[]{:S(2)}) async-start(bf16[8,256,128]{2,1,0:T(8,128)(2,1)} %pack.1.start.previous), calls=%async_computation.1 | async-start | bytes 1048576 | tf_op jit(solution)/shard_map/all_to_all | solution.py:599
  30.9 1.4 %collective-permute-done.5.handed = s32[2048]{0:T(1024)S(1)} collective-permute-done((s32[2048]{0:T(1024)}, s32[2048]{0:T(1024)S(1)}, u32[]{:S(2)}, u32[]{:S(2)}) %collective-permute-start.5) | collective-permute-done | bytes 8224 | tf_op jit(solution)/shard_map/ppermute | solution.py:603
  32.3 0.7 copy-done
  33.0 1.2 %settle.1.plan = s32[2048]{0:T(1024)S(4)} custom-call(s32[2]{0:T(128)S(1)} %pad_add_fusion.place, s32[2048]{0:T(1024)S(1)} %copy-done, s32[2048]{0:T(1024)S(1)} %collective-permute-done.5.handed), custom_call_target="tpu_custom_call" | custom-call | tf_op jit(solution)/shard_map/settle/pallas_call | solution.py:513
  34.2 6.8 %all-to-all-done.1.pieces.q1 = bf16[8,256,128]{2,1,0:T(8,128)(2,1)S(1)} async-done(((bf16[8,256,128]{2,1,0:T(8,128)(2,1)}), bf16[8,256,128]{2,1,0:T(8,128)(2,1)S(1)}, u32[]{:S(2)}, u32[]{:S(2)}) %all-to-all-start.1) | async-done | bytes 524320 | tf_op jit(solution)/shard_map/all_to_all | solution.py:599
  41.0 3.4 %sent.2 = (bf16[8,256,128]{2,1,0:T(8,128)(2,1)S(1)}, bf16[66,256,256]{2,1,0:T(8,128)(2,1)S(1)}) custom-call(s32[2048]{0:T(1024)S(4)} %settle.1.plan, bf16[32,256,256]{2,1,0:T(8,128)(2,1)} %bitcast.23, bf16[32,256,256]{2,1,0:T(8,128)(2,1)} %collective-permute-done.6.tile_b, bf16[8,256,128]{2,1,0:T(8,128)(2,1)S(1)} %all-to-all-done.1.pieces.q1, ...), custom_call_target="tpu_custom_call" | custom-call | flops 134217728 | bytes 2621440 | tf_op jit(solution)/shard_map/sent/pallas_call | solution.py:513
  44.4 13.2 %all_to_all.24.pieces.q2 = bf16[8,256,128]{2,1,0:T(8,128)(2,1)S(1)} all-to-all(bf16[8,256,128]{2,1,0:T(8,128)(2,1)S(1)} %get-tuple-element.34.current), channel_id=1, replica_groups=mesh['row'=8,'col'=2,'vec'=2] {'row'}, dimensions={0} | all-to-all | bytes 1048576 | tf_op jit(solution)/shard_map/all_to_all | solution.py:710
  57.5 2.5 %sent.3 = bf16[8,256,128]{2,1,0:T(8,128)(2,1)} custom-call(s32[2048]{0:T(1024)S(4)} %settle.1.plan, bf16[66,256,256]{2,1,0:T(8,128)(2,1)S(1)} %get-tuple-element.33.blocks, bf16[8,256,128]{2,1,0:T(8,128)(2,1)S(1)} %all_to_all.24.pieces.q2, bf16[8,256,128]{2,1,0:T(8,128)(2,1)S(1)} %get-tuple-element.34.current, bf16[8,256,128]{2,1,0:T(8,128)(2,1)} %pack.1.start.previous), custom_call_target="tpu_custom_call" | custom-call | flops 134217728 | bytes 2621440 | tf_op jit(solution)/shard_map/sent/pallas_call | solution.py:513
  60.1 3.5 %all-to-all-start.3 = ((bf16[8,256,128]{2,1,0:T(8,128)(2,1)}), bf16[8,256,128]{2,1,0:T(8,128)(2,1)S(1)}, u32[]{:S(2)}, u32[]{:S(2)}) async-start(bf16[8,256,128]{2,1,0:T(8,128)(2,1)} %sent.3), calls=%async_computation.3 | async-start | bytes 1048576 | tf_op jit(solution)/shard_map/all_to_all | solution.py:715
  63.6 0.5 collective-permute-start.8
  64.1 1.4 %collective-permute-done.7.q1_other = bf16[8,256,128]{2,1,0:T(8,128)(2,1)S(1)} collective-permute-done((bf16[8,256,128]{2,1,0:T(8,128)(2,1)S(1)}, bf16[8,256,128]{2,1,0:T(8,128)(2,1)S(1)}, u32[]{:S(2)}, u32[]{:S(2)}) %collective-permute-start.7) | collective-permute-done | bytes 524320 | tf_op jit(solution)/shard_map/ppermute | solution.py:712
  65.5 0.7 collective-permute-done.8.q2_other
  66.3 8.4 %early.1.array = bf16[32,256,128]{2,1,0:T(8,128)(2,1)} custom-call(s32[2048]{0:T(1024)S(4)} %settle.1.plan, bf16[32,256,256]{2,1,0:T(8,128)(2,1)} %bitcast.24, bf16[32,256,256]{2,1,0:T(8,128)(2,1)} %collective-permute-done.6.tile_b, bf16[8,256,128]{2,1,0:T(8,128)(2,1)S(1)} %all-to-all-done.1.pieces.q1, ...), custom_call_target="tpu_custom_call" | custom-call | flops 1073741824 | bytes 20971520 | tf_op jit(solution)/shard_map/early/pallas_call | solution.py:513
  74.7 0.2 collective-permute-start.9
  74.9 2.5 %load.1 = (bf16[36,256,256]{2,1,0:T(8,128)(2,1)S(1)}, bf16[32,256,128]{2,1,0:T(8,128)(2,1)S(1)}) custom-call(s32[2048]{0:T(1024)S(4)} %settle.1.plan, bf16[32,256,256]{2,1,0:T(8,128)(2,1)} %bitcast.25, bf16[32,256,128]{2,1,0:T(8,128)(2,1)} %early.1.array), custom_call_target="tpu_custom_call" | custom-call | tf_op jit(solution)/shard_map/load/pallas_call | solution.py:513
  77.3 4.8 %last.1 = bf16[32,256,128]{2,1,0:T(8,128)(2,1)} custom-call(s32[2048]{0:T(1024)S(4)} %settle.1.plan, bf16[36,256,256]{2,1,0:T(8,128)(2,1)S(1)} %get-tuple-element.39.blocks, bf16[32,256,256]{2,1,0:T(8,128)(2,1)} %collective-permute-done.6.tile_b, bf16[8,256,128]{2,1,0:T(8,128)(2,1)S(1)} %all-to-all-done.3.mine, ...), custom_call_target="tpu_custom_call" | custom-call | flops 536870912 | bytes 10485760 | tf_op jit(solution)/shard_map/last/pallas_call | solution.py:513
  (21 shorter events, 0.9 us)
Async XLA Ops:
  0.0 19.8 %copy-start.1 = (s32[1,1,32]{2,1,0:T(1,128)S(1)}, s32[1,1,32]{2,1,0:T(1,128)}, u32[]{:S(2)}) copy-start(s32[1,1,32]{2,1,0:T(1,128)} %param.8) | copy-start | bytes 388
  0.0 19.8 %copy-start.2 = (s32[1,1,32]{2,1,0:T(1,128)S(1)}, s32[1,1,32]{2,1,0:T(1,128)}, u32[]{:S(2)}) copy-start(s32[1,1,32]{2,1,0:T(1,128)} %param.7) | copy-start | bytes 388
  0.0 41.0 %collective-permute-start.6 = (bf16[32,256,256]{2,1,0:T(8,128)(2,1)}, bf16[32,256,256]{2,1,0:T(8,128)(2,1)}, u32[]{:S(2)}, u32[]{:S(2)}) collective-permute-start(bf16[32,256,256]{2,1,0:T(8,128)(2,1)} %bitcast.22), channel_id=1, source_target_pairs={{0,2},{2,0},{1,3},{3,1},{4,6},{6,4},{5,7},{7,5},{8,10},{10,8},{9,1... | collective-permute-start | bytes 12582920 | tf_op jit(solution)/shard_map/ppermute | solution.py:568
  16.2 2.0 %collective-permute-start.1 = (bf16[8,256,128]{2,1,0:T(8,128)(2,1)S(1)}, bf16[8,256,128]{2,1,0:T(8,128)(2,1)S(1)}, u32[]{:S(2)}, u32[]{:S(2)}) collective-permute-start(bf16[8,256,128]{2,1,0:T(8,128)(2,1)S(1)} %pick.1.picked), channel_id=1, source_target_pairs={{0,2},{2,0},{1,3},{3,1},{4,6},{6,4},{5,7},{7,5},{8,10},{10,8},{9,1... | collective-permute-start | bytes 1572872 | tf_op jit(solution)/shard_map/ppermute | solution.py:569
  16.3 3.5 %collective-permute-start = (s32[8,128]{1,0:T(8,128)S(1)}, s32[8,128]{1,0:T(8,128)S(1)}, u32[]{:S(2)}, u32[]{:S(2)}) collective-permute-start(s32[8,128]{1,0:T(8,128)S(1)} %bitcast.16), channel_id=1, source_target_pairs={{0,2},{2,0},{1,3},{3,1},{4,6},{6,4},{5,7},{7,5},{8,10},{10,8},{9,1... | collective-permute-start | bytes 12296 | tf_op jit(solution)/shard_map/ppermute | solution.py:570
  17.5 2.3 %collective-permute-start.2 = (s32[32]{0:T(128)}, s32[32]{0:T(128)S(1)}, u32[]{:S(2)}, u32[]{:S(2)}) collective-permute-start(s32[32]{0:T(128)} %bitcast.20), channel_id=1, source_target_pairs={{0,2},{2,0},{1,3},{3,1},{4,6},{6,4},{5,7},{7,5},{8,10},{10,8},{9,1... | collective-permute-start | bytes 392 | tf_op jit(solution)/shard_map/ppermute | solution.py:572
  17.6 2.2 %collective-permute-start.3 = (s32[32]{0:T(128)}, s32[32]{0:T(128)S(1)}, u32[]{:S(2)}, u32[]{:S(2)}) collective-permute-start(s32[32]{0:T(128)} %bitcast.18), channel_id=1, source_target_pairs={{0,2},{2,0},{1,3},{3,1},{4,6},{6,4},{5,7},{7,5},{8,10},{10,8},{9,1... | collective-permute-start | bytes 392 | tf_op jit(solution)/shard_map/ppermute | solution.py:572
  18.2 1.6 %collective-permute-start.4 = (s32[1]{0:T(128)}, s32[1]{0:T(128)}, u32[]{:S(2)}, u32[]{:S(2)}) collective-permute-start(s32[1]{0:T(128)} %bitcast.5), channel_id=1, source_target_pairs={{0,2},{2,0},{1,3},{3,1},{4,6},{6,4},{5,7},{7,5},{8,10},{10,8},{9,1... | collective-permute-start | bytes 20 | tf_op jit(solution)/shard_map/ppermute | solution.py:572
  27.3 13.7 %all-to-all-start.1 = ((bf16[8,256,128]{2,1,0:T(8,128)(2,1)}), bf16[8,256,128]{2,1,0:T(8,128)(2,1)S(1)}, u32[]{:S(2)}, u32[]{:S(2)}) async-start(bf16[8,256,128]{2,1,0:T(8,128)(2,1)} %pack.1.start.previous), calls=%async_computation.1 | async-start | bytes 1048576 | tf_op jit(solution)/shard_map/all_to_all | solution.py:599
  30.8 1.4 %collective-permute-start.5 = (s32[2048]{0:T(1024)}, s32[2048]{0:T(1024)S(1)}, u32[]{:S(2)}, u32[]{:S(2)}) collective-permute-start(s32[2048]{0:T(1024)} %get-tuple-element.30), channel_id=1, source_target_pairs={{0,2},{2,0},{1,3},{3,1},{4,6},{6,4},{5,7},{7,5},{8,10},{10,8},{9,1... | collective-permute-start | bytes 24584 | tf_op jit(solution)/shard_map/ppermute | solution.py:603
  32.3 0.7 copy-start
  60.1 14.6 %all-to-all-start.3 = ((bf16[8,256,128]{2,1,0:T(8,128)(2,1)}), bf16[8,256,128]{2,1,0:T(8,128)(2,1)S(1)}, u32[]{:S(2)}, u32[]{:S(2)}) async-start(bf16[8,256,128]{2,1,0:T(8,128)(2,1)} %sent.3), calls=%async_computation.3 | async-start | bytes 1048576 | tf_op jit(solution)/shard_map/all_to_all | solution.py:715
  63.6 2.0 %collective-permute-start.7 = (bf16[8,256,128]{2,1,0:T(8,128)(2,1)S(1)}, bf16[8,256,128]{2,1,0:T(8,128)(2,1)S(1)}, u32[]{:S(2)}, u32[]{:S(2)}) collective-permute-start(bf16[8,256,128]{2,1,0:T(8,128)(2,1)S(1)} %all-to-all-done.1.pieces.q1), channel_id=1, source_target_pairs={{0,2},{2,0},{1,3},{3,1},{4,6},{6,4},{5,7},{7,5},{8,10},{10,8},{9,1... | collective-permute-start | bytes 1572872 | tf_op jit(solution)/shard_map/ppermute | solution.py:712
  63.6 2.6 %collective-permute-start.8 = (bf16[8,256,128]{2,1,0:T(8,128)(2,1)S(1)}, bf16[8,256,128]{2,1,0:T(8,128)(2,1)S(1)}, u32[]{:S(2)}, u32[]{:S(2)}) collective-permute-start(bf16[8,256,128]{2,1,0:T(8,128)(2,1)S(1)} %all_to_all.24.pieces.q2), channel_id=1, source_target_pairs={{0,2},{2,0},{1,3},{3,1},{4,6},{6,4},{5,7},{7,5},{8,10},{10,8},{9,1... | collective-permute-start | bytes 1572872 | tf_op jit(solution)/shard_map/ppermute | solution.py:713
  74.7 2.7 %collective-permute-start.9 = (bf16[8,256,128]{2,1,0:T(8,128)(2,1)S(1)}, bf16[8,256,128]{2,1,0:T(8,128)(2,1)S(1)}, u32[]{:S(2)}, u32[]{:S(2)}) collective-permute-start(bf16[8,256,128]{2,1,0:T(8,128)(2,1)S(1)} %all-to-all-done.3.mine), channel_id=1, source_target_pairs={{0,2},{2,0},{1,3},{3,1},{4,6},{6,4},{5,7},{7,5},{8,10},{10,8},{9,1... | collective-permute-start | bytes 1572872 | tf_op jit(solution)/shard_map/ppermute | solution.py:716

commit v3 on v0

--- a/solution.py
+++ b/solution.py
@@ -83,6 +83,7 @@
 
     def scan(tile, meta):
         used = meta[2 * slot_count]
+
 
         def step(s, carry):
             ends, sent, load = carry
@@ -370,19 +371,32 @@
 
     @pl.when(half == 0)
     def _():
-        @pl.loop(0, n_row)
-        def _(p):
+        for p in range(n_row):
             one, two = mine[p], other[p]
             vec[0, p, :, at : at + width] = jnp.concatenate([one[:, :middle], two[:, middle:]], axis=1)
             vec[1, p, :, at : at + width] = jnp.concatenate([one[:, middle:], two[:, :middle]], axis=1)
 
     @pl.when(half != 0)
     def _():
-        @pl.loop(0, n_row)
-        def _(p):
+        for p in range(n_row):
             one, two = mine[p], other[p]
             vec[0, p, :, at : at + width] = jnp.concatenate([two[:, middle:], one[:, :middle]], axis=1)
             vec[1, p, :, at : at + width] = jnp.concatenate([two[:, :middle], one[:, middle:]], axis=1)
+
+
+def prime_kernel(vectors, total, own, sem):
+    _, block_size, double = total.shape
+    width = double // 2
+    copy = pltpu.make_async_copy(vectors, own, sem)
+    copy.start()
+    copy.wait()
+
+    @pl.loop(0, vectors.shape[0] // block_size)
+    def _(b):
+        at = pl.ds(pl.multiple_of(b * block_size, block_size), block_size)
+        value = own[at, :].astype(jnp.float32)
+        total[b, :, :width] = -center_value * value
+        total[b, :, width:] = -value
 
 
 def early_kernel(
@@ -394,37 +408,26 @@
     q1_other,
     q2,
     q2_other,
-    vectors,
+    start,
     base,
+    total,
     vec,
-    total,
     own,
     blocks,
-    sem,
     sems,
     row_sems,
 ):
-    width = vectors.shape[1]
-    piece_blocks, block_size, _ = base.shape
-    copy = pltpu.make_async_copy(vectors, own, sem)
-    copy.start()
+    piece_blocks, block_size, width = base.shape
     begin, wait = fetches(plan, HEAD, STRIDE, 0, lay.slots, (tile_a, tile_b), blocks, sems)
     begin()
     whole_columns(plan[7], q1, q1_other, vec, 0)
     whole_columns(plan[7], q2, q2_other, vec, width)
-    copy.wait()
 
     def rows(b):
         return pl.ds(pl.multiple_of(b * block_size, block_size), block_size)
 
     def put(b):
         return pltpu.make_async_copy(own.at[rows(b)], base.at[b], row_sems.at[b])
-
-    @pl.loop(0, piece_blocks)
-    def _(b):
-        value = own[rows(b), :].astype(jnp.float32)
-        total[b, :, :width] = -center_value * value
-        total[b, :, width:] = -value
 
     add_products(
         plan,
@@ -507,7 +510,7 @@
     return lax.optimization_barrier((value, *others))[0]
 
 
-def call(kernel, out, args, spaces, scratch, mib, name, estimate=None):
+def call(kernel, out, args, spaces, scratch, mib, name, estimate=None, aliases=None):
     args = [
         pltpu.with_memory_space_constraint(arg, space) if space in (VMEM, HBM) or tied else arg
         for arg, (space, tied) in zip(args, spaces)
@@ -520,6 +523,7 @@
         scratch_shapes=scratch,
         compiler_params=params(mib),
         cost_estimate=estimate,
+        input_output_aliases=aliases or {},
         name=name,
     )(*args)
 
@@ -556,9 +560,7 @@
     exchange = functools.partial(
         lax.all_to_all, axis_name="row", split_axis=0, concat_axis=0, tiled=True
     )
-    meta = jnp.concatenate([slot_rows, slot_cols, used])
-    meta_other = across(meta)
-    wanted = after(exchange(jnp.broadcast_to(needed, (n_row, LANES))), meta_other, place)
+    wanted = exchange(jnp.broadcast_to(needed, (n_row, LANES)))
     sent_shape = (n_row, block_size, width)
     (sent,) = call(
         functools.partial(pick_kernel, n_row, block_size),
@@ -572,6 +574,8 @@
     tile_other = across(tile)
     sent_other = across(sent)
     wanted_other = across(after(wanted, sent))
+    meta = jnp.concatenate([slot_rows, slot_cols, used])
+    meta_other = across(after(meta, sent))
     packed = call(
         pack_kernel,
         [(sent_shape, jnp.bfloat16, HBM)],
@@ -667,24 +671,25 @@
 
     base_shape = (piece_blocks, block_size, width)
 
+    sums_shape = ((piece_blocks + 1, block_size, 2 * width), jnp.float32, VMEM)
+
     def early(*args):
         return call(
             functools.partial(early_kernel, lay),
-            [(base_shape, jnp.bfloat16, HBM)],
+            [(base_shape, jnp.bfloat16, HBM), sums_shape],
             (plan, tile, tile_other, *args),
-            (LIST, FAR, ANYWHERE, HERE, HERE, HERE, HERE, FAR),
+            (LIST, FAR, ANYWHERE, HERE, HERE, HERE, HERE, HERE),
             [
                 VMEM((2, n_row, block_size, 2 * width), jnp.bfloat16),
-                VMEM((piece_blocks + 1, block_size, 2 * width), jnp.float32),
                 VMEM(vectors.shape, jnp.bfloat16),
                 VMEM((2 * lay.slots, block_size, block_size), jnp.bfloat16),
-                DMA,
                 DMA((2 * lay.slots,)),
                 DMA((piece_blocks,)),
             ],
-            28,
+            18,
             "early",
             cost(2 * slot_count, 2 * piece_blocks),
+            {7: 1},
         )[0]
 
     def last(blocks, *args):
@@ -714,7 +719,17 @@
     second_sent = second_blocks(blocks, q2, first_sent, packed)
     q1_other = across(after(q1, second_sent))
     q2_other = across(after(q2, second_sent))
-    base = early(q1, q1_other, q2, q2_other, vectors)
+    (start,) = call(
+        prime_kernel,
+        [sums_shape],
+        (after(vectors, second_sent),),
+        (FAR,),
+        [VMEM(vectors.shape, jnp.bfloat16), DMA],
+        4,
+        "prime",
+        cost(0, 3 * piece_blocks),
+    )
+    base = early(q1, q1_other, q2, q2_other, start)
     q3 = after(exchange(second_sent), base)
     q3_other = across(q3)
     blocks, base = load(q3, base)

time: 83.9 us -> 86.9 us (1.036)
  blocking collectives: 15.1 us -> 31.1 us
  starting transfers between devices: 15.8 us -> 9.78 us
  waiting for transfers between devices: 20.4 us -> 15.9 us
  Pallas kernels: 28.3 us -> 26.2 us
    all_to_all x0 -> x1, blocking collectives: none -> 13.1 us  [on_pair(): wanted = exchange(jnp.broadcast_to(needed, (n_row, LANES)))]
    all_to_all x1 -> x0, starting transfers between devices: 6.8 us -> none  [on_pair(): exchange(jnp.broadcast_to(needed, (n_row, LANES)))]
    all_to_all x1 -> x0, waiting for transfers between devices: 3.86 us -> none  [on_pair(): exchange(jnp.broadcast_to(needed, (n_row, LANES)))]
    all_to_all x1, waiting for transfers between devices: 3.36 us -> 6.4 us  [on_pair(): q3 = after(exchange(second_sent), base)]
    all_to_all x1, blocking collectives: 15.1 us -> 18.1 us  [on_pair(): q2 = exchange(first_sent)]
    pallas_call x9 -> x10, Pallas kernels: 28.3 us -> 26.2 us  [call(): pl.pallas_call(kernel, out_shape=[space(shape, dtype) for shape, dtype, s...]
    ppermute x1, waiting for transfers between devices: 1.4 us -> 0.01 us  [on_pair(): sent_other = across(sent)]
    ppermute x1, waiting for transfers between devices: 1.4 us -> 0.01 us  [on_pair(): q1_other = across(after(q1, second_sent))]
  transfers between devices with their start and end apart: 11 -> 10, of which waited for: 8 -> 3; matrix products, arithmetic and copies ran while one was open for 3% -> 2% of each run, Pallas kernels for 22% -> 21%
where the time goes in v3:
time: 86.9 us; the launch traced here: 86.1 us
  blocking collectives  31.1 us (36%)
  Pallas kernels  26.2 us (30%)
  waiting for transfers between devices  15.9 us (18%)
  starting transfers between devices  9.78 us (11%)
  other arithmetic  1.61 us (2%)
    pallas_call x10, Pallas kernels, call(): pl.pallas_call(kernel, out_shape=[space(shape, dtype) for shape, dtype, s...  26.2 us
    all_to_all x1, blocking collectives, on_pair(): q2 = exchange(first_sent)  18.1 us
    all_to_all x1, blocking collectives, on_pair(): wanted = exchange(jnp.broadcast_to(needed, (n_row, LANES)))  13.1 us
    all_to_all x1, waiting for transfers between devices, on_pair(): q1 = exchange(after(packed, own_list))  8.07 us
    all_to_all x1, waiting for transfers between devices, on_pair(): q3 = after(exchange(second_sent), base)  6.4 us
    all_to_all x1, starting transfers between devices, on_pair(): q3 = after(exchange(second_sent), base)  4.66 us
    all_to_all x1, starting transfers between devices, on_pair(): q1 = exchange(after(packed, own_list))  3.51 us
  transfers between devices with their start and end apart: 10, of which 3 were waited for; matrix products, arithmetic and copies ran while one was open for 2% of the time, Pallas kernels for 21%

profile of v3, /device:TPU:0, one launch (start us, length us, event | category | flops | bytes accessed | tf_op | source)
XLA Modules:
  0.0 86.1 jit_solution(14590448478083387804)
XLA Ops:
  0.0 0.5 collective-permute-start.4
  0.5 0.7 and_select_fusion.1
  1.1 0.1 select_reduce_fusion
  1.3 13.1 %all_to_all.23 = s32[8,1,128]{2,1,0:T(1,128)S(1)} all-to-all(s32[8,1,128]{2,1,0:T(1,128)S(1)} %broadcast_in_dim.21), channel_id=1, replica_groups=mesh['row'=8,'col'=2,'vec'=2] {'row'}, dimensions={0} | all-to-all | bytes 8192 | tf_op jit(solution)/shard_map/all_to_all | solution.py:563
  14.4 1.7 %pick.1.picked = bf16[8,256,128]{2,1,0:T(8,128)(2,1)S(1)} custom-call(s32[8,128]{1,0:T(8,128)S(1)} %bitcast.15, bf16[8192,128]{1,0:T(8,128)(2,1)} %vectors.2), custom_call_target="tpu_custom_call" | custom-call | tf_op jit(solution)/shard_map/pick/pallas_call | solution.py:518
  16.9 0.5 collective-permute-start
  17.4 0.7 pad_add_fusion.1.meta_a
  18.2 1.5 %pack.1.start.previous = bf16[8,256,128]{2,1,0:T(8,128)(2,1)} custom-call(s32[2]{0:T(128)S(1)} %pad_add_fusion.place, bf16[8,256,128]{2,1,0:T(8,128)(2,1)S(1)} %pick.1.picked, bf16[8,256,128]{2,1,0:T(8,128)(2,1)S(1)} %collective-permute-done.1.picked_b), custom_call_target="tpu_custom_call" | custom-call | tf_op jit(solution)/shard_map/pack/pallas_call | solution.py:518
  19.7 4.6 %plan.1 = (s32[2048]{0:T(1024)}, s32[2048]{0:T(1024)}) custom-call(s32[2]{0:T(128)S(1)} %pad_add_fusion.place, s32[8,128]{1,0:T(8,128)S(1)} %bitcast.17, s32[8,128]{1,0:T(8,128)S(1)} %collective-permute-done.wanted_b, s32[65]{0:T(128)S(1)} %pad_add_fusion.1.meta_a, s32[65]{0:T(128)S(1)} %collective-permute-done.2.meta_b), custom_call_target="tpu_custom_call" | custom-call | tf_op jit(solution)/shard_map/plan/pallas_call | solution.py:518
  24.3 3.5 %all-to-all-start.1 = ((bf16[8,256,128]{2,1,0:T(8,128)(2,1)}), bf16[8,256,128]{2,1,0:T(8,128)(2,1)S(1)}, u32[]{:S(2)}, u32[]{:S(2)}) async-start(bf16[8,256,128]{2,1,0:T(8,128)(2,1)} %pack.1.start.previous), calls=%async_computation.1 | async-start | bytes 1048576 | tf_op jit(solution)/shard_map/all_to_all | solution.py:606
  27.9 1.4 %collective-permute-done.3.handed = s32[2048]{0:T(1024)S(1)} collective-permute-done((s32[2048]{0:T(1024)}, s32[2048]{0:T(1024)S(1)}, u32[]{:S(2)}, u32[]{:S(2)}) %collective-permute-start.3) | collective-permute-done | bytes 8224 | tf_op jit(solution)/shard_map/ppermute | solution.py:610
  29.3 0.7 copy-done
  30.0 1.2 %settle.1.plan = s32[2048]{0:T(1024)S(4)} custom-call(s32[2]{0:T(128)S(1)} %pad_add_fusion.place, s32[2048]{0:T(1024)S(1)} %copy-done, s32[2048]{0:T(1024)S(1)} %collective-permute-done.3.handed), custom_call_target="tpu_custom_call" | custom-call | tf_op jit(solution)/shard_map/settle/pallas_call | solution.py:518
  31.2 8.1 %all-to-all-done.1.pieces.q1 = bf16[8,256,128]{2,1,0:T(8,128)(2,1)S(1)} async-done(((bf16[8,256,128]{2,1,0:T(8,128)(2,1)}), bf16[8,256,128]{2,1,0:T(8,128)(2,1)S(1)}, u32[]{:S(2)}, u32[]{:S(2)}) %all-to-all-start.1) | async-done | bytes 524320 | tf_op jit(solution)/shard_map/all_to_all | solution.py:606
  39.3 2.6 %sent.2 = (bf16[8,256,128]{2,1,0:T(8,128)(2,1)S(1)}, bf16[66,256,256]{2,1,0:T(8,128)(2,1)S(1)}) custom-call(s32[2048]{0:T(1024)S(4)} %settle.1.plan, bf16[32,256,256]{2,1,0:T(8,128)(2,1)} %bitcast.19, bf16[32,256,256]{2,1,0:T(8,128)(2,1)} %collective-permute-done.4.tile_b, bf16[8,256,128]{2,1,0:T(8,128)(2,1)S(1)} %all-to-all-done.1.pieces.q1, ...), custom_call_target="tpu_custom_call" | custom-call | flops 134217728 | bytes 2621440 | tf_op jit(solution)/shard_map/sent/pallas_call | solution.py:518
  41.9 18.1 %all_to_all.24.pieces.q2 = bf16[8,256,128]{2,1,0:T(8,128)(2,1)S(1)} all-to-all(bf16[8,256,128]{2,1,0:T(8,128)(2,1)S(1)} %get-tuple-element.32.current), channel_id=1, replica_groups=mesh['row'=8,'col'=2,'vec'=2] {'row'}, dimensions={0} | all-to-all | bytes 1048576 | tf_op jit(solution)/shard_map/all_to_all | solution.py:718
  60.0 2.1 %sent.3 = bf16[8,256,128]{2,1,0:T(8,128)(2,1)} custom-call(s32[2048]{0:T(1024)S(4)} %settle.1.plan, bf16[66,256,256]{2,1,0:T(8,128)(2,1)S(1)} %get-tuple-element.31.blocks, bf16[8,256,128]{2,1,0:T(8,128)(2,1)S(1)} %all_to_all.24.pieces.q2, bf16[8,256,128]{2,1,0:T(8,128)(2,1)S(1)} %get-tuple-element.32.current, bf16[8,256,128]{2,1,0:T(8,128)(2,1)} %pack.1.start.previous), custom_call_target="tpu_custom_call" | custom-call | flops 134217728 | bytes 2621440 | tf_op jit(solution)/shard_map/sent/pallas_call | solution.py:518
  62.1 4.7 %all-to-all-start.3 = ((bf16[8,256,128]{2,1,0:T(8,128)(2,1)}), bf16[8,256,128]{2,1,0:T(8,128)(2,1)S(1)}, u32[]{:S(2)}, u32[]{:S(2)}) async-start(bf16[8,256,128]{2,1,0:T(8,128)(2,1)} %sent.3), calls=%async_computation.3 | async-start | bytes 1048576 | tf_op jit(solution)/shard_map/all_to_all | solution.py:733
  66.7 0.5 collective-permute-start.6
  67.2 2.3 %prime.1.start = f32[33,256,256]{2,1,0:T(8,128)S(1)} custom-call(bf16[8192,128]{1,0:T(8,128)(2,1)} %vectors.2), custom_call_target="tpu_custom_call" | custom-call | bytes 18874368 | tf_op jit(solution)/shard_map/prime/pallas_call | solution.py:518
  69.6 4.8 %early.1 = (bf16[32,256,128]{2,1,0:T(8,128)(2,1)}, f32[33,256,256]{2,1,0:T(8,128)S(1)}) custom-call(s32[2048]{0:T(1024)S(4)} %settle.1.plan, bf16[32,256,256]{2,1,0:T(8,128)(2,1)} %bitcast.20, bf16[32,256,256]{2,1,0:T(8,128)(2,1)} %collective-permute-done.4.tile_b, ...), custom_call_target="tpu_custom_call", output_to_operand_aliasing={{1}: (7, {})} | custom-call | flops 1073741824 | bytes 20971520 | tf_op jit(solution)/shard_map/early/pallas_call | solution.py:518
  74.4 6.4 %all-to-all-done.3.mine = bf16[8,256,128]{2,1,0:T(8,128)(2,1)S(1)} async-done(((bf16[8,256,128]{2,1,0:T(8,128)(2,1)}), bf16[8,256,128]{2,1,0:T(8,128)(2,1)S(1)}, u32[]{:S(2)}, u32[]{:S(2)}) %all-to-all-start.3) | async-done | bytes 524320 | tf_op jit(solution)/shard_map/all_to_all | solution.py:733
  80.8 2.0 %load.1 = (bf16[36,256,256]{2,1,0:T(8,128)(2,1)S(1)}, bf16[32,256,128]{2,1,0:T(8,128)(2,1)S(1)}) custom-call(s32[2048]{0:T(1024)S(4)} %settle.1.plan, bf16[32,256,256]{2,1,0:T(8,128)(2,1)} %bitcast.21, bf16[32,256,128]{2,1,0:T(8,128)(2,1)} %get-tuple-element.36.array), custom_call_target="tpu_custom_call" | custom-call | tf_op jit(solution)/shard_map/load/pallas_call | solution.py:518
  82.8 3.3 %last.1 = bf16[32,256,128]{2,1,0:T(8,128)(2,1)} custom-call(s32[2048]{0:T(1024)S(4)} %settle.1.plan, bf16[36,256,256]{2,1,0:T(8,128)(2,1)S(1)} %get-tuple-element.39.blocks, bf16[32,256,256]{2,1,0:T(8,128)(2,1)} %collective-permute-done.4.tile_b, bf16[8,256,128]{2,1,0:T(8,128)(2,1)S(1)} %all-to-all-done.3.mine, ...), custom_call_target="tpu_custom_call" | custom-call | flops 536870912 | bytes 10485760 | tf_op jit(solution)/shard_map/last/pallas_call | solution.py:518
  (15 shorter events, 0.3 us)
Async XLA Ops:
  0.0 39.3 %collective-permute-start.4 = (bf16[32,256,256]{2,1,0:T(8,128)(2,1)}, bf16[32,256,256]{2,1,0:T(8,128)(2,1)}, u32[]{:S(2)}, u32[]{:S(2)}) collective-permute-start(bf16[32,256,256]{2,1,0:T(8,128)(2,1)} %bitcast.18), channel_id=1, source_target_pairs={{0,2},{2,0},{1,3},{3,1},{4,6},{6,4},{5,7},{7,5},{8,10},{10,8},{9,1... | collective-permute-start | bytes 12582920 | tf_op jit(solution)/shard_map/ppermute | solution.py:574
  16.1 2.1 %collective-permute-start.1 = (bf16[8,256,128]{2,1,0:T(8,128)(2,1)S(1)}, bf16[8,256,128]{2,1,0:T(8,128)(2,1)S(1)}, u32[]{:S(2)}, u32[]{:S(2)}) collective-permute-start(bf16[8,256,128]{2,1,0:T(8,128)(2,1)S(1)} %pick.1.picked), channel_id=1, source_target_pairs={{0,2},{2,0},{1,3},{3,1},{4,6},{6,4},{5,7},{7,5},{8,10},{10,8},{9,1... | collective-permute-start | bytes 1572872 | tf_op jit(solution)/shard_map/ppermute | solution.py:575
  16.9 2.8 %collective-permute-start = (s32[8,128]{1,0:T(8,128)S(1)}, s32[8,128]{1,0:T(8,128)S(1)}, u32[]{:S(2)}, u32[]{:S(2)}) collective-permute-start(s32[8,128]{1,0:T(8,128)S(1)} %bitcast.16), channel_id=1, source_target_pairs={{0,2},{2,0},{1,3},{3,1},{4,6},{6,4},{5,7},{7,5},{8,10},{10,8},{9,1... | collective-permute-start | bytes 12296 | tf_op jit(solution)/shard_map/ppermute | solution.py:576
  18.2 1.5 %collective-permute-start.2 = (s32[65]{0:T(128)S(1)}, s32[65]{0:T(128)S(1)}, u32[]{:S(2)}, u32[]{:S(2)}) collective-permute-start(s32[65]{0:T(128)S(1)} %pad_add_fusion.1.meta_a), channel_id=1, source_target_pairs={{0,2},{2,0},{1,3},{3,1},{4,6},{6,4},{5,7},{7,5},{8,10},{10,8},{9,1... | collective-permute-start | bytes 788 | tf_op jit(solution)/shard_map/ppermute | solution.py:578
  24.3 15.0 %all-to-all-start.1 = ((bf16[8,256,128]{2,1,0:T(8,128)(2,1)}), bf16[8,256,128]{2,1,0:T(8,128)(2,1)S(1)}, u32[]{:S(2)}, u32[]{:S(2)}) async-start(bf16[8,256,128]{2,1,0:T(8,128)(2,1)} %pack.1.start.previous), calls=%async_computation.1 | async-start | bytes 1048576 | tf_op jit(solution)/shard_map/all_to_all | solution.py:606
  27.8 1.4 %collective-permute-start.3 = (s32[2048]{0:T(1024)}, s32[2048]{0:T(1024)S(1)}, u32[]{:S(2)}, u32[]{:S(2)}) collective-permute-start(s32[2048]{0:T(1024)} %get-tuple-element.28), channel_id=1, source_target_pairs={{0,2},{2,0},{1,3},{3,1},{4,6},{6,4},{5,7},{7,5},{8,10},{10,8},{9,1... | collective-permute-start | bytes 24584 | tf_op jit(solution)/shard_map/ppermute | solution.py:610
  29.3 0.7 copy-start
  62.1 18.7 %all-to-all-start.3 = ((bf16[8,256,128]{2,1,0:T(8,128)(2,1)}), bf16[8,256,128]{2,1,0:T(8,128)(2,1)S(1)}, u32[]{:S(2)}, u32[]{:S(2)}) async-start(bf16[8,256,128]{2,1,0:T(8,128)(2,1)} %sent.3), calls=%async_computation.3 | async-start | bytes 1048576 | tf_op jit(solution)/shard_map/all_to_all | solution.py:733
  66.7 2.8 %collective-permute-start.5 = (bf16[8,256,128]{2,1,0:T(8,128)(2,1)S(1)}, bf16[8,256,128]{2,1,0:T(8,128)(2,1)S(1)}, u32[]{:S(2)}, u32[]{:S(2)}) collective-permute-start(bf16[8,256,128]{2,1,0:T(8,128)(2,1)S(1)} %all-to-all-done.1.pieces.q1), channel_id=1, source_target_pairs={{0,2},{2,0},{1,3},{3,1},{4,6},{6,4},{5,7},{7,5},{8,10},{10,8},{9,1... | collective-permute-start | bytes 1572872 | tf_op jit(solution)/shard_map/ppermute | solution.py:720
  66.7 2.8 %collective-permute-start.6 = (bf16[8,256,128]{2,1,0:T(8,128)(2,1)S(1)}, bf16[8,256,128]{2,1,0:T(8,128)(2,1)S(1)}, u32[]{:S(2)}, u32[]{:S(2)}) collective-permute-start(bf16[8,256,128]{2,1,0:T(8,128)(2,1)S(1)} %all_to_all.24.pieces.q2), channel_id=1, source_target_pairs={{0,2},{2,0},{1,3},{3,1},{4,6},{6,4},{5,7},{7,5},{8,10},{10,8},{9,1... | collective-permute-start | bytes 1572872 | tf_op jit(solution)/shard_map/ppermute | solution.py:721
  80.8 2.0 %collective-permute-start.7 = (bf16[8,256,128]{2,1,0:T(8,128)(2,1)S(1)}, bf16[8,256,128]{2,1,0:T(8,128)(2,1)S(1)}, u32[]{:S(2)}, u32[]{:S(2)}) collective-permute-start(bf16[8,256,128]{2,1,0:T(8,128)(2,1)S(1)} %all-to-all-done.3.mine), channel_id=1, source_target_pairs={{0,2},{2,0},{1,3},{3,1},{4,6},{6,4},{5,7},{7,5},{8,10},{10,8},{9,1... | collective-permute-start | bytes 1572872 | tf_op jit(solution)/shard_map/ppermute | solution.py:734
